TPU v7x, 32 devices: a whole 2x2x4 slice. The times are simulated.
32 devices in a mesh: dp: 4 (over x, core), context: 2 (over y), expert: 4 (over z).
Axes of the slice: x: 2, y: 2, z: 4, core: 2. Of those that a mesh axis runs over, the one named last changes fastest.
Arguments:
- tokens: bfloat16 [4, 512, 2048], P('dp', 'context'), may hold values from -6 to 6
- norm1_gain: bfloat16 [2048], P(('dp', 'context')), may hold values from 0.5 to 1.5
- w_qkv: bfloat16 [2048, 3, 2048], P(('dp', 'context'), None, 'expert'), may hold values from -0.125 to 0.125
- b_qkv: bfloat16 [3, 16, 128], P(None, 'expert'), may hold values from -1.1953125 to 1.1953125
- w_out: bfloat16 [2048, 2048], P('expert', ('dp', 'context')), may hold values from -0.5 to 0.5
- norm2_gain: bfloat16 [2048], P(('dp', 'context')), may hold values from 0.5 to 1.5
- w_router: bfloat16 [2048, 8], P(('dp', 'context')), may hold values from -0.0625 to 0.0625
- shared_gate: bfloat16 [2048], P(('dp', 'context')), may hold values from -0.125 to 0.125
- w_shared_in: bfloat16 [2048, 2, 5632], P(('dp', 'context'), None, 'expert'), may hold values from -0.125 to 0.125
- w_shared_out: bfloat16 [5632, 2048], P('expert', ('dp', 'context')), may hold values from -0.15625 to 0.15625
- w_expert_in: bfloat16 [8, 2048, 2, 1408], P(('context', 'expert'), 'dp'), may hold values from -0.125 to 0.125
- w_expert_out: bfloat16 [8, 1408, 2048], P(('context', 'expert'), None, 'dp'), may hold values from -0.3125 to 0.3125
- block_ids: int32 [4, 512], P('dp'), may hold values from 0 to 3, never falling along the last dimension, each value on 1 to 256 neighbouring positions
- expert_ids: int32 [4, 512, 4], P('dp', ('context', 'expert')), may hold values from 0 to 7, all different within a row; in each aligned block of 64 rows (0 to 63, 64 to 127, ..., all dimensions but the last counted through in order) at most 48 rows name the same one
- out_grad: bfloat16 [4, 512, 2048], P('dp', 'context'), may hold values from -6 to 6
Outputs:
- output: bfloat16 [4, 512, 2048], P('dp', ('context', 'expert'))
- grad_tokens: bfloat16 [4, 512, 2048], P('dp', ('context', 'expert'))
- grad_norm1_gain: bfloat16 [2048], P(('dp', 'context'))
- grad_w_qkv: bfloat16 [2048, 3, 2048], P(('dp', 'context'), None, 'expert')
- grad_b_qkv: bfloat16 [3, 16, 128], P(None, 'expert', ('dp', 'context'))
- grad_w_out: bfloat16 [2048, 2048], P('expert', ('dp', 'context'))
- grad_norm2_gain: bfloat16 [2048], P(('dp', 'context'))
- grad_w_router: bfloat16 [2048, 8], P(('dp', 'context'))
- grad_shared_gate: bfloat16 [2048], P(('dp', 'context'))
- grad_w_shared_in: bfloat16 [2048, 2, 5632], P(('dp', 'context'), None, 'expert')
- grad_w_shared_out: bfloat16 [5632, 2048], P('expert', ('dp', 'context'))
- grad_w_expert_in: bfloat16 [8, 2048, 2, 1408], P(('context', 'expert'), 'dp')
- grad_w_expert_out: bfloat16 [8, 1408, 2048], P(('context', 'expert'), None, 'dp')
Inputs may be any that keep to these rules, and one draw needn't show every extreme that they name: `expert_ids`: each row names 4 different experts. In each aligned block of 64 rows (the rows of one device in order of sequence and position) no expert is named by more than 48 rows, a bound that some block reaches. `block_ids`: within a sequence the block number never falls; each block holds 1 to 256 positions, one exactly 256.
All inputs are finite; a program needn't handle non-finite values.
Results may differ from a plain program's by a relative error of at most 0.035.
Values may be sent and summed in bfloat16 or wider, within the bound.
A program may use at most 256 MiB of HBM per device.

v0:
```python
from types import SimpleNamespace

import jax
import jax.numpy as jnp
import numpy as np
from jax import lax
from jax.experimental import pallas as pl
from jax.experimental.pallas import tpu as pltpu
from jax.sharding import PartitionSpec as P

highest = lax.Precision.HIGHEST
epsilon = 1e-06
rope_base = 1000000.0
f32 = jnp.float32
bf16 = jnp.bfloat16
DP, CTX, EXP = "dp", "context", "expert"
PLANE, GROUP = (DP, CTX), (CTX, EXP)


def rotary_tables(first_row, row_count, head_size):
    exponent = jnp.arange(head_size // 2).astype(jnp.float32) * (2.0 / head_size)
    frequency = rope_base ** (-exponent)
    positions = (first_row + jnp.arange(row_count, dtype=jnp.int32)).astype(jnp.float32)
    angles = positions[:, None] * frequency[None, :]
    return (jnp.cos(angles)[:, None, :], jnp.sin(angles)[:, None, :])


def rotate(values, cosine, sine_table):
    half_size = values.shape[-1] // 2
    first_half = values[..., :half_size]
    second_half = values[..., half_size:]
    return jnp.concatenate(
        [
            first_half * cosine - second_half * sine_table,
            second_half * cosine + first_half * sine_table,
        ],
        axis=-1,
    )


def rotate_back(grad_values, cosine, sine_table):
    half_size = grad_values.shape[-1] // 2
    first_half = grad_values[..., :half_size]
    second_half = grad_values[..., half_size:]
    return jnp.concatenate(
        [
            first_half * cosine + second_half * sine_table,
            second_half * cosine - first_half * sine_table,
        ],
        axis=-1,
    )


def gated_grads(gate_part, up_part, grad_act):
    sigmoid_gate = jax.nn.sigmoid(gate_part)
    grad_gate = grad_act * up_part * sigmoid_gate * (1.0 + gate_part * (1.0 - sigmoid_gate))
    grad_up = grad_act * gate_part * sigmoid_gate
    return (grad_gate, grad_up)


def masked_scores(queries, all_keys, allowed, score_scale):
    scores = (
        jnp.einsum("qhd,khd->hqk", queries, all_keys, preferred_element_type=jnp.float32)
        * score_scale
    )
    return jnp.where(allowed[None], scores, -1e30)


def fetch_dense(
    norm1_gain, w_qkv, w_out, norm2_gain, w_router, shared_gate, w_shared_in, w_shared_out
):
    return (
        lax.all_gather(norm1_gain, PLANE, axis=0, tiled=True),
        lax.all_gather(w_qkv, PLANE, axis=0, tiled=True),
        lax.all_gather(w_out, PLANE, axis=1, tiled=True),
        lax.all_gather(norm2_gain, PLANE, axis=0, tiled=True),
        lax.all_gather(w_router, PLANE, axis=0, tiled=True),
        lax.all_gather(shared_gate, PLANE, axis=0, tiled=True),
        lax.all_gather(w_shared_in, PLANE, axis=0, tiled=True),
        lax.all_gather(w_shared_out, PLANE, axis=1, tiled=True),
    )


def fetch_experts(w_expert_in, w_expert_out):
    return (
        lax.all_gather(w_expert_in, DP, axis=1, tiled=True),
        lax.all_gather(w_expert_out, DP, axis=2, tiled=True),
    )


def fetch_keys(key_rows, value_rows):
    return (
        lax.all_gather(key_rows, CTX, axis=0, tiled=True),
        lax.all_gather(value_rows, CTX, axis=0, tiled=True),
    )


def general_body(
    tokens,
    norm1_gain,
    w_qkv,
    b_qkv,
    w_out,
    norm2_gain,
    w_router,
    shared_gate,
    w_shared_in,
    w_shared_out,
    w_expert_in,
    w_expert_out,
    block_ids,
    expert_ids,
    out_grad,
):
    token_rows = tokens[0]
    rows_local, model_width = token_rows.shape
    lane_count = lax.axis_size(EXP)
    quarter = rows_local // lane_count
    first_row = lax.axis_index(CTX) * rows_local
    own_row = lax.axis_index(EXP) * quarter
    sequence_ids = block_ids[0]
    chosen = expert_ids[0]
    top_count = chosen.shape[1]
    heads_local = b_qkv.shape[1]
    head_size = b_qkv.shape[2]
    dense_full = fetch_dense(
        norm1_gain, w_qkv, w_out, norm2_gain, w_router, shared_gate, w_shared_in, w_shared_out
    )
    (
        gain_one,
        qkv_weight,
        out_weight,
        gain_two,
        router_weight,
        gate_vector,
        shared_in,
        shared_out,
    ) = dense_full
    expert_pair = fetch_experts(w_expert_in, w_expert_out)
    expert_in = expert_pair[0][0]
    expert_back = expert_pair[1][0]
    ffe_width = expert_in.shape[2]
    experts = router_weight.shape[1]
    capacity = max(2, 3 * quarter * top_count // (2 * experts))
    tokens_wide = token_rows.astype(jnp.float32)
    inverse_one = lax.rsqrt(jnp.mean(tokens_wide * tokens_wide, axis=-1, keepdims=True) + epsilon)
    normed = (tokens_wide * inverse_one * gain_one.astype(jnp.float32)).astype(jnp.bfloat16)
    linear = jnp.dot(
        normed, qkv_weight.reshape(model_width, -1), preferred_element_type=jnp.float32
    )
    linear = linear.reshape(rows_local, 3, heads_local, head_size) + b_qkv.astype(jnp.float32)[None]
    cosine, sine_table = rotary_tables(first_row, rows_local, head_size)
    queries = rotate(linear[:, 0], cosine, sine_table).astype(jnp.bfloat16)
    key_rows = rotate(linear[:, 1], cosine, sine_table).astype(jnp.bfloat16)
    value_rows = linear[:, 2].astype(jnp.bfloat16)
    all_keys, all_values = fetch_keys(key_rows, value_rows)
    query_ids = lax.dynamic_slice_in_dim(sequence_ids, first_row, rows_local)
    allowed = sequence_ids[None, :] <= query_ids[:, None]
    score_scale = head_size ** (-0.5)
    scores = masked_scores(queries, all_keys, allowed, score_scale)
    row_peak = jnp.max(scores, axis=-1, keepdims=True)
    log_total = row_peak + jnp.log(jnp.sum(jnp.exp(scores - row_peak), axis=-1, keepdims=True))
    weights = jnp.exp(scores - log_total).astype(jnp.bfloat16)
    attended = jnp.einsum("hqk,khd->qhd", weights, all_values, preferred_element_type=jnp.float32)
    attended_low = attended.astype(jnp.bfloat16).reshape(rows_local, heads_local * head_size)
    attention = lax.psum(
        jnp.dot(attended_low, out_weight, preferred_element_type=jnp.float32).astype(jnp.bfloat16),
        EXP,
    ).astype(jnp.float32)
    hidden = tokens_wide + attention
    inverse_two = lax.rsqrt(jnp.mean(hidden * hidden, axis=-1, keepdims=True) + epsilon)
    routed = (hidden * inverse_two * gain_two.astype(jnp.float32)).astype(jnp.bfloat16)
    shared_up = jnp.dot(
        routed, shared_in.reshape(model_width, -1), preferred_element_type=jnp.float32
    )
    shared_up = shared_up.reshape(rows_local, 2, -1)
    shared_act = (jax.nn.silu(shared_up[:, 0]) * shared_up[:, 1]).astype(jnp.bfloat16)
    shared_part = jnp.dot(shared_act, shared_out, preferred_element_type=jnp.float32)
    shared_rows = lax.psum_scatter(
        shared_part.astype(jnp.bfloat16), EXP, scatter_dimension=0, tiled=True
    ).astype(jnp.float32)
    shared_weight = jax.nn.sigmoid(jnp.dot(routed, gate_vector, preferred_element_type=jnp.float32))
    routed_own = lax.dynamic_slice_in_dim(routed, own_row, quarter)
    hidden_own = lax.dynamic_slice_in_dim(hidden, own_row, quarter)
    weight_own = lax.dynamic_slice_in_dim(shared_weight, own_row, quarter)
    logits = jnp.dot(routed_own, router_weight, preferred_element_type=jnp.float32)
    probability = jax.nn.softmax(logits, axis=-1)
    expert_match = (chosen[..., None] == jnp.arange(experts, dtype=jnp.int32)).astype(jnp.float32)
    gate_values = jnp.sum(probability[:, None, :] * expert_match, axis=-1)
    flat_ids = chosen.reshape(-1)
    onehot = (flat_ids[:, None] == jnp.arange(experts, dtype=jnp.int32)).astype(jnp.int32)
    slot_rank = jnp.sum((jnp.cumsum(onehot, axis=0) - onehot) * onehot, axis=-1)
    slot_index = flat_ids * capacity + slot_rank
    placement = (slot_index[:, None] == jnp.arange(experts * capacity, dtype=jnp.int32)).astype(
        jnp.bfloat16
    )
    repeated = jnp.repeat(routed_own, top_count, axis=0)
    outgoing = jnp.einsum("sr,sd->rd", placement, repeated, preferred_element_type=jnp.float32)
    outgoing = outgoing.astype(jnp.bfloat16).reshape(experts, capacity, model_width)
    incoming = lax.all_to_all(
        outgoing, GROUP, split_axis=0, concat_axis=0, tiled=True
    )
    flat_rows = incoming.reshape(-1, model_width)
    gate_up = jnp.dot(
        flat_rows, expert_in.reshape(model_width, -1), preferred_element_type=jnp.float32
    ).reshape(-1, 2, ffe_width)
    activated = (jax.nn.silu(gate_up[:, 0]) * gate_up[:, 1]).astype(jnp.bfloat16)
    result = jnp.dot(activated, expert_back, preferred_element_type=jnp.float32).astype(
        jnp.bfloat16
    )
    expert_result = result.reshape(incoming.shape)
    returned = lax.all_to_all(
        expert_result, GROUP, split_axis=0, concat_axis=0, tiled=True
    )
    picked = jnp.dot(
        placement, returned.reshape(-1, model_width), preferred_element_type=jnp.float32
    )
    picked = picked.reshape(quarter, top_count, model_width)
    combined = jnp.sum(gate_values[..., None] * picked, axis=1)
    result_rows = hidden_own + combined + weight_own[:, None] * shared_rows
    output = result_rows.astype(jnp.bfloat16)[None]
    (
        gain_one_b,
        qkv_weight_b,
        out_weight_b,
        gain_two_b,
        router_weight_b,
        gate_vector_b,
        shared_in_b,
        shared_out_b,
    ) = dense_full
    expert_in_b = expert_pair[0][0]
    expert_back_b = expert_pair[1][0]
    grad_full = out_grad[0].astype(jnp.float32)
    grad_own = lax.dynamic_slice_in_dim(grad_full, own_row, quarter)
    shared_grad = (shared_weight[:, None] * grad_full).astype(jnp.bfloat16)
    grad_shared_out = jnp.einsum(
        "tf,td->fd", shared_act, shared_grad, preferred_element_type=jnp.float32
    )
    grad_shared_act = jnp.einsum(
        "td,fd->tf", shared_grad, shared_out_b, preferred_element_type=jnp.float32
    )
    shared_gate_grad, shared_up_grad = gated_grads(
        shared_up[:, 0], shared_up[:, 1], grad_shared_act
    )
    grad_shared_up = jnp.stack([shared_gate_grad, shared_up_grad], axis=1).astype(jnp.bfloat16)
    grad_shared_in = jnp.einsum(
        "td,tkf->dkf", routed, grad_shared_up, preferred_element_type=jnp.float32
    )
    grad_routed = jnp.einsum(
        "tkf,dkf->td", grad_shared_up, shared_in_b, preferred_element_type=jnp.float32
    )
    gate_slope = jnp.sum(grad_own * shared_rows, axis=-1) * weight_own * (1.0 - weight_own)
    grad_gate_vector = jnp.dot(gate_slope, routed_own.astype(jnp.float32), precision=highest)
    grad_own_routed = gate_slope[:, None] * gate_vector_b.astype(jnp.float32)[None]
    grad_gates = jnp.sum(grad_own[:, None, :] * picked, axis=-1)
    grad_slots = (
        (gate_values[..., None] * grad_own[:, None, :])
        .astype(jnp.bfloat16)
        .reshape(-1, model_width)
    )
    grad_send = jnp.einsum("sr,sd->rd", placement, grad_slots, preferred_element_type=jnp.float32)
    grad_send = grad_send.astype(jnp.bfloat16).reshape(experts, capacity, model_width)
    grad_arrived = lax.all_to_all(
        grad_send, GROUP, split_axis=0, concat_axis=0, tiled=True
    )
    arrived_rows = incoming.reshape(-1, model_width)
    arrived_grad = grad_arrived.reshape(-1, model_width)
    expert_up = jnp.dot(
        arrived_rows, expert_in_b.reshape(model_width, -1), preferred_element_type=jnp.float32
    ).reshape(-1, 2, ffe_width)
    expert_act = (jax.nn.silu(expert_up[:, 0]) * expert_up[:, 1]).astype(jnp.bfloat16)
    grad_expert_back = jnp.einsum(
        "rf,rd->fd", expert_act, arrived_grad, preferred_element_type=jnp.float32
    )
    grad_expert_act = jnp.einsum(
        "rd,fd->rf", arrived_grad, expert_back_b, preferred_element_type=jnp.float32
    )
    expert_gate_grad, expert_up_grad = gated_grads(
        expert_up[:, 0], expert_up[:, 1], grad_expert_act
    )
    grad_expert_up = jnp.stack([expert_gate_grad, expert_up_grad], axis=1).astype(jnp.bfloat16)
    grad_expert_in = jnp.einsum(
        "rd,rkf->dkf", arrived_rows, grad_expert_up, preferred_element_type=jnp.float32
    )
    grad_arrived_rows = jnp.einsum(
        "rkf,dkf->rd", grad_expert_up, expert_in_b, preferred_element_type=jnp.float32
    )
    grad_arrived_rows = grad_arrived_rows.astype(jnp.bfloat16).reshape(
        experts, capacity, model_width
    )
    grad_returned = lax.all_to_all(
        grad_arrived_rows, GROUP, split_axis=0, concat_axis=0, tiled=True
    )
    grad_copies = jnp.dot(
        placement, grad_returned.reshape(-1, model_width), preferred_element_type=jnp.float32
    )
    grad_own_routed = grad_own_routed + jnp.sum(
        grad_copies.reshape(quarter, top_count, model_width), axis=1
    )
    grad_probability = jnp.sum(grad_gates[..., None] * expert_match, axis=1)
    grad_logits = probability * (
        grad_probability - jnp.sum(probability * grad_probability, axis=-1, keepdims=True)
    )
    grad_router = jnp.dot(routed_own.astype(jnp.float32).T, grad_logits, precision=highest)
    grad_own_routed = grad_own_routed + jnp.dot(
        grad_logits, router_weight_b.astype(jnp.float32).T, precision=highest
    )
    own_part = lax.dynamic_slice_in_dim(grad_routed, own_row, quarter) + grad_own_routed
    grad_routed = lax.dynamic_update_slice_in_dim(grad_routed, own_part, own_row, 0)
    grad_routed, grad_router, grad_gate_vector = (
        lax.psum(grad_routed.astype(jnp.bfloat16), EXP).astype(jnp.float32),
        lax.psum(grad_router.astype(jnp.bfloat16), EXP).astype(jnp.float32),
        lax.psum(grad_gate_vector.astype(jnp.bfloat16), EXP).astype(jnp.float32),
    )
    scaled_two = grad_routed * gain_two_b.astype(jnp.float32)
    grad_gain_two = jnp.sum(grad_routed * hidden * inverse_two, axis=0)
    grad_hidden = (
        grad_full
        + inverse_two * scaled_two
        - hidden * inverse_two**3 * jnp.mean(scaled_two * hidden, axis=-1, keepdims=True)
    )
    grad_hidden_low = grad_hidden.astype(jnp.bfloat16)
    grad_out_weight = jnp.einsum(
        "tn,td->nd", attended_low, grad_hidden_low, preferred_element_type=jnp.float32
    )
    grad_attended = jnp.einsum(
        "td,nd->tn", grad_hidden_low, out_weight_b, preferred_element_type=jnp.float32
    )
    grad_attended = grad_attended.astype(jnp.bfloat16).reshape(rows_local, heads_local, head_size)
    back_keys, back_values = (all_keys, all_values)
    scores_again = masked_scores(queries, back_keys, allowed, score_scale)
    weights_wide = jnp.exp(scores_again - log_total)
    row_delta = jnp.sum(grad_attended.astype(jnp.float32) * attended, axis=-1).T
    grad_weights = jnp.einsum(
        "qhd,khd->hqk", grad_attended, back_values, preferred_element_type=jnp.float32
    )
    grad_scores = (weights_wide * (grad_weights - row_delta[..., None])).astype(jnp.bfloat16)
    grad_queries = (
        jnp.einsum("hqk,khd->qhd", grad_scores, back_keys, preferred_element_type=jnp.float32)
        * score_scale
    )
    grad_keys = (
        jnp.einsum("hqk,qhd->khd", grad_scores, queries, preferred_element_type=jnp.float32)
        * score_scale
    )
    grad_values = jnp.einsum(
        "hqk,qhd->khd",
        weights_wide.astype(jnp.bfloat16),
        grad_attended,
        preferred_element_type=jnp.float32,
    )
    grad_keys, grad_values = (
        lax.psum_scatter(
            grad_keys.astype(jnp.bfloat16), CTX, scatter_dimension=0, tiled=True
        ).astype(jnp.float32),
        lax.psum_scatter(
            grad_values.astype(jnp.bfloat16), CTX, scatter_dimension=0, tiled=True
        ).astype(jnp.float32),
    )
    grad_linear = jnp.stack(
        [
            rotate_back(grad_queries, cosine, sine_table),
            rotate_back(grad_keys, cosine, sine_table),
            grad_values,
        ],
        axis=1,
    )
    grad_linear = grad_linear.astype(jnp.bfloat16)
    grad_bias = jnp.sum(grad_linear.astype(jnp.float32), axis=0)
    grad_flat = grad_linear.reshape(rows_local, -1)
    grad_qkv = jnp.einsum(
        "td,tn->dn", normed, grad_flat, preferred_element_type=jnp.float32
    ).reshape(qkv_weight_b.shape)
    grad_normed = jnp.einsum(
        "tn,dn->td",
        grad_flat,
        qkv_weight_b.reshape(model_width, -1),
        preferred_element_type=jnp.float32,
    )
    grad_normed = lax.psum(grad_normed.astype(jnp.bfloat16), EXP).astype(jnp.float32)
    scaled_one = grad_normed * gain_one_b.astype(jnp.float32)
    grad_gain_one = jnp.sum(grad_normed * tokens_wide * inverse_one, axis=0)
    grad_tokens = (
        grad_hidden
        + inverse_one * scaled_one
        - tokens_wide * inverse_one**3 * jnp.mean(scaled_one * tokens_wide, axis=-1, keepdims=True)
    )
    grad_tokens_own = lax.dynamic_slice_in_dim(grad_tokens, own_row, quarter).astype(jnp.bfloat16)[
        None
    ]
    dense_sums = (
        lax.psum_scatter(
            grad_gain_one.astype(jnp.bfloat16), PLANE, scatter_dimension=0, tiled=True
        ).astype(jnp.float32),
        lax.psum_scatter(
            grad_qkv.astype(jnp.bfloat16), PLANE, scatter_dimension=0, tiled=True
        ).astype(jnp.float32),
        lax.psum_scatter(
            grad_bias.astype(jnp.bfloat16), PLANE, scatter_dimension=2, tiled=True
        ).astype(jnp.float32),
        lax.psum_scatter(
            grad_out_weight.astype(jnp.bfloat16), PLANE, scatter_dimension=1, tiled=True
        ).astype(jnp.float32),
        lax.psum_scatter(
            grad_gain_two.astype(jnp.bfloat16), PLANE, scatter_dimension=0, tiled=True
        ).astype(jnp.float32),
        lax.psum_scatter(
            grad_router.astype(jnp.bfloat16), PLANE, scatter_dimension=0, tiled=True
        ).astype(jnp.float32),
        lax.psum_scatter(
            grad_gate_vector.astype(jnp.bfloat16),
            PLANE,
            scatter_dimension=0,
            tiled=True,
        ).astype(jnp.float32),
        lax.psum_scatter(
            grad_shared_in.astype(jnp.bfloat16), PLANE, scatter_dimension=0, tiled=True
        ).astype(jnp.float32),
        lax.psum_scatter(
            grad_shared_out.astype(jnp.bfloat16), PLANE, scatter_dimension=1, tiled=True
        ).astype(jnp.float32),
    )
    expert_sums = (
        lax.psum_scatter(
            grad_expert_in[None].astype(jnp.bfloat16), DP, scatter_dimension=1, tiled=True
        ).astype(jnp.float32),
        lax.psum_scatter(
            grad_expert_back[None].astype(jnp.bfloat16), DP, scatter_dimension=2, tiled=True
        ).astype(jnp.float32),
    )
    return (
        output,
        grad_tokens_own,
        dense_sums[0].astype(jnp.bfloat16),
        dense_sums[1].astype(jnp.bfloat16),
        dense_sums[2].astype(jnp.bfloat16),
        dense_sums[3].astype(jnp.bfloat16),
        dense_sums[4].astype(jnp.bfloat16),
        dense_sums[5].astype(jnp.bfloat16),
        dense_sums[6].astype(jnp.bfloat16),
        dense_sums[7].astype(jnp.bfloat16),
        dense_sums[8].astype(jnp.bfloat16),
        expert_sums[0].astype(jnp.bfloat16),
        expert_sums[1].astype(jnp.bfloat16),
    )


MIB = 1 << 20
MESH = pl.DeviceIdType.MESH


def dot_nn(a, b):
    return lax.dot_general(a, b, (((1,), (0,)), ((), ())), preferred_element_type=f32)


def dot_nt(a, b):
    return lax.dot_general(a, b, (((1,), (1,)), ((), ())), preferred_element_type=f32)


def dot_tn(a, b):
    return lax.dot_general(a, b, (((0,), (0,)), ((), ())), preferred_element_type=f32)


def place():
    i = lax.axis_index(DP)
    return i // 2, i % 2, lax.axis_index(CTX), lax.axis_index(EXP)


def owner_dense(r):
    x, c, y, _ = place()
    return (((x + r % 2) % 2) * 2 + (c + r // 4) % 2) * 2 + (y + (r // 2) % 2) % 2


def owner_expert(r):
    x, c, _, _ = place()
    return ((x + r % 2) % 2) * 2 + (c + r // 2) % 2


def near(d):
    z = lax.axis_index(EXP)
    return ((z // 2 + d // 2) % 2) * 2 + (z % 2 + d % 2) % 2


def peers():
    x, c, y, _ = place()
    far = [{EXP: near(d)} for d in (1, 2, 3)]
    return {DP: ((x + 1) % 2) * 2 + c}, {CTX: 1 - y}, {DP: x * 2 + (c + 1) % 2}, far


def greet(devices):
    barrier = pltpu.get_barrier_semaphore()
    for device in devices:
        pl.semaphore_signal(barrier, 1, device_id=device, device_id_type=MESH)
    pl.semaphore_wait(barrier, len(devices))


class Wire:
    def __init__(self, wires, ends, device):
        self.ends, self.device, self.sent = ends, device, False
        self.send, self.recv, self.k = wires.send, wires.recv, len(wires.copies)
        wires.copies.append(self)

    def copy(self):
        source, target = self.ends()
        return pltpu.make_async_remote_copy(
            src_ref=source,
            dst_ref=target,
            send_sem=self.send.at[self.k],
            recv_sem=self.recv.at[self.k],
            device_id=self.device,
            device_id_type=MESH,
        )

    def start(self):
        self.copy().start()
        return self

    def wait_recv(self):
        self.copy().wait_recv()

    def wait_send(self):
        self.copy().wait_send()
        self.sent = True


class Wires:
    def __init__(self, send, recv):
        self.send, self.recv, self.copies = send, recv, []

    def add(self, ends, device):
        return Wire(self, ends, device)

    def go(self, ends, device):
        return Wire(self, ends, device).start()

    def drain(self):
        for wire in self.copies:
            if not wire.sent:
                wire.wait_send()


class Loads:
    def __init__(self, sems):
        self.sems, self.count = sems, 0

    def go(self, source, target):
        copy = pltpu.make_async_copy(source, target, self.sems.at[self.count])
        self.count += 1
        copy.start()
        return copy


def cols(ref, block, width):
    return ref[:, pl.ds(pl.multiple_of(block * width, width), width)]


def piece(ref, d, rows):
    return ref[pl.ds(pl.multiple_of(near(d) * rows, rows), rows), :]


def turn(values, cosine, sine):
    return values * cosine + pltpu.roll(values, 64, 1) * sine


def turn_back(values, cosine, sine):
    return values * cosine - pltpu.roll(values, 64, 1) * sine


def gated(gate, up, grad_act):
    s = jax.nn.sigmoid(gate)
    act = gate * s
    return act * up, grad_act * up * s * (1.0 + gate * (1.0 - s)), grad_act * act


def softmax_parts(q, k_own, k_oth, mask_own, mask_oth):
    scale = 128 ** (-0.5)
    s_own = jnp.where(mask_own, dot_nt(q, k_own) * scale, -1e30)
    s_oth = jnp.where(mask_oth, dot_nt(q, k_oth) * scale, -1e30)
    peak = jnp.maximum(
        jnp.max(s_own, axis=-1, keepdims=True), jnp.max(s_oth, axis=-1, keepdims=True)
    )
    e_own = jnp.exp(s_own - peak)
    e_oth = jnp.exp(s_oth - peak)
    total = jnp.sum(e_own, axis=-1, keepdims=True) + jnp.sum(e_oth, axis=-1, keepdims=True)
    back = 1.0 / total
    return e_own * back, e_oth * back


def split3(v):
    high = v.astype(bf16).astype(f32)
    mid = (v - high).astype(bf16).astype(f32)
    return high, mid, v - high - mid


def probabilities(rows, small):
    logits = dot_nt(rows, small[...])
    lane = lax.broadcasted_iota(jnp.int32, logits.shape, 1)
    logits = jnp.where((lane >= 3) & (lane < 11), logits, -1e30)
    e = jnp.exp(logits - jnp.max(logits, axis=-1, keepdims=True))
    return e / jnp.sum(e, axis=-1, keepdims=True), lane


ARRIVAL = (0, 4, 1, 5, 2, 6, 3, 7)


class Spread:
    def __init__(self, wires, own, slots, dense):
        x, y, core, _ = peers()
        self.slots, self.own, self.copies = slots, own, {}

        def ends(r, target):
            return lambda: (self.block(r), slots.at[target])

        self.copies[1] = wires.add(ends(0, 1), x)
        if dense:
            self.copies[2] = wires.add(ends(0, 2), y)
            self.copies[3] = wires.add(ends(1, 3), y)
        side = 4 if dense else 2
        for r in range(side):
            self.copies[side + r] = wires.add(ends(r, side + r), core)

    def block(self, r):
        return self.own() if r == 0 else self.slots.at[r]

    def start(self, r):
        self.copies[r].start()

    def wait(self, r):
        self.copies[r].wait_recv()


V, A = "vmem", "any"


def call(kernel, number, ins, outs, scratch, vmem, flops, traffic):
    def spec(kind):
        return pl.BlockSpec(memory_space=pl.ANY if kind == A else pltpu.VMEM)

    names = list(ins) + list(outs) + list(scratch)

    def run(*refs):
        kernel(SimpleNamespace(**dict(zip(names, refs))))

    made = pl.pallas_call(
        run,
        out_shape=tuple(jax.ShapeDtypeStruct(o[0], o[1]) for o in outs.values()),
        in_specs=[spec(i[1]) for i in ins.values()],
        out_specs=tuple(spec(o[2]) for o in outs.values()),
        scratch_shapes=list(scratch.values()),
        compiler_params=pltpu.CompilerParams(
            vmem_limit_bytes=vmem * MIB, collective_id=number, has_side_effects=number is not None
        ),
        cost_estimate=pl.CostEstimate(flops=flops, bytes_accessed=traffic, transcendentals=0),
    )(*[i[0] for i in ins.values()])
    return SimpleNamespace(**dict(zip(outs, made)))


def own_rows(total, hidden, routed, g, small, high_o, low_o, vec_o):
    extra = total[:, 2048:2176]
    wide = routed.astype(f32)
    prob, _ = probabilities(routed, small)
    sw = jax.nn.sigmoid(jnp.sum(wide * small[2:3, :].astype(f32), axis=-1, keepdims=True))
    slope = jnp.sum(extra[:, 48:96], axis=-1, keepdims=True) * sw * (1.0 - sw)
    dgate = [
        extra[:, e : e + 1] + extra[:, 16 + e : 17 + e] + extra[:, 32 + e : 33 + e]
        for e in range(8)
    ]
    probs = [prob[:, 3 + e : 4 + e] for e in range(8)]
    mean = sum(p * d for p, d in zip(probs, dgate))
    grad = total[:, 0:2048] + slope * small[2:3, :].astype(f32)
    vec_o[...] = jnp.zeros_like(vec_o)
    vec_o[2:3, :] = jnp.sum(slope * wide, axis=0, keepdims=True)
    for e in range(8):
        dlogit = probs[e] * (dgate[e] - mean)
        grad += dlogit * small[3 + e : 4 + e, :].astype(f32)
        vec_o[3 + e : 4 + e, :] = jnp.sum(dlogit * wide, axis=0, keepdims=True)
    inv = lax.rsqrt(jnp.mean(hidden * hidden, axis=-1, keepdims=True) + epsilon)
    vec_o[1:2, :] = jnp.sum(grad * hidden * inv, axis=0, keepdims=True)
    scaled = grad * small[1:2, :].astype(f32)
    mean = jnp.mean(scaled * hidden, axis=-1, keepdims=True)
    high = g.astype(f32) + inv * scaled - hidden * (inv * inv * inv * mean)
    high_o[...] = high
    low_o[...] = high.astype(bf16)


def layer_kernel(k):
    x_dev, y_dev, core_dev, z_dev = peers()
    wires, loads = Wires(k.send_sems, k.recv_sems), Loads(k.load_sems)
    greet([x_dev, y_dev, core_dev] + z_dev)
    y = lax.axis_index(CTX)
    mine = y * 4 + lax.axis_index(EXP)

    def to_z(make):
        return [wires.go(make(d), z_dev[d - 1]) for d in (1, 2, 3)]

    class Collect:
        def __init__(self, slot):
            self.slot = slot
            self.one = wires.go(lambda: (slot(0), slot(1)), z_dev[0])
            self.three = wires.go(lambda: (slot(0), slot(3)), z_dev[2])

        def hand_on(self):
            self.three.wait_recv()
            self.two = wires.go(lambda: (self.slot(3), self.slot(2)), z_dev[0])

        def wait(self):
            self.one.wait_recv()
            self.two.wait_recv()

    vec = Spread(wires, lambda: k.w_v, k.s_v, True)
    qkv = Spread(wires, lambda: k.w_q, k.s_q, True)
    out = Spread(wires, lambda: k.w_o, k.s_o, True)
    eg = Spread(wires, lambda: k.split_ei.at[0], k.s_eg, False)
    eu = Spread(wires, lambda: k.split_ei.at[1], k.s_eu, False)
    ed = Spread(wires, lambda: k.w_ed, k.s_ed, False)
    sg = Spread(wires, lambda: k.split_si.at[0], k.s_sg, True)
    su = Spread(wires, lambda: k.split_si.at[1], k.s_su, True)
    sd = Spread(wires, lambda: k.w_sd, k.s_sd, True)
    first, expert, shared = (vec, qkv), (eg, eu, ed), (sg, su, sd)
    k.w_v[...] = jnp.zeros_like(k.w_v)
    for m, vector in enumerate((k.gain_one, k.gain_two, k.gate_vector)):
        k.w_v[m : m + 1, :] = vector[...].reshape(1, 256)
    k.w_v[3:11, :] = k.router[...]
    for s in first + (out, ed):
        s.start(1)
    for s in first:
        s.start(2)
    for s in first + (out,):
        s.start(4)
    k.col[0:128, :] = jnp.full((128, 128), -1.0, f32)
    k.col[0:4, 0:64] = k.ids_own[...].astype(f32)
    k.ids[0, 0:64, :] = k.col[0:128, :].T[0:64, :]
    ids_y = wires.go(lambda: (k.ids.at[0, pl.ds(0, 64), :], k.ids_y), y_dev)
    k.s_v[0] = k.w_v[...]
    k.col[...] = jnp.broadcast_to(k.blocks[...].astype(f32), (128, 512)).T
    for target, half in ((k.ids_near, y), (k.ids_far, 1 - y)):
        for d in range(4):
            at = pl.ds(pl.multiple_of(half * 256 + near(d) * 64, 64), 64)
            k.ids_q[d * 64 : (d + 1) * 64, :] = k.col[at, :]
        target[...] = k.ids_q[...].T[0:8, :]
    for d in range(4):
        at = pl.ds(pl.multiple_of(y * 256 + near(d) * 64, 64), 64)
        to = slice(d * 64, (d + 1) * 64)
        k.ids_q[to, :] = k.col[at, :]
        k.cs[to, :] = k.cs_all[at, :]
        k.sn[to, :] = k.sn_all[at, :]
    later = []

    def attention_part(scaled, acc, w, low_w, mixed, apart):
        held, held_out = {}, []

        def bring(r):
            held[r] = loads.go(qkv.block(r), w.at[r])

        def bring_out(r):
            held_out.append(loads.go(out.block(r), low_w.at[r]))

        raw = [loads.go(k.w_ei.at[pl.ds(256 * m, 256)], mixed.at[m]) for m in range(2)]
        raw.append(loads.go(k.w_si, mixed.at[2]))
        bring(0)
        for d in range(4):
            t = piece(k.tok, d, 64).astype(f32)
            inv = lax.rsqrt(jnp.mean(t * t, axis=-1, keepdims=True) + epsilon)
            scaled[d * 64 : (d + 1) * 64, :] = t * inv
            k.inv1[d * 64 : (d + 1) * 64, :] = inv
        for m in range(3):
            for h in range(4):
                at = slice(h * 128, (h + 1) * 128)
                line = k.bias[m, h : h + 1, :].astype(f32)
                acc[m, :, at] = jnp.broadcast_to(line, (256, 128))

        def take_apart(m):
            raw[m].wait()
            target = k.split_si if m == 2 else k.split_ei
            to = pl.ds(0 if m == 2 else 256 * m, 256)
            done = []
            for n in range(2):
                apart[m, n] = mixed[m, :, n, :]
                done.append(loads.go(apart.at[m, n], target.at[n, to, :]))
            return done

        done = take_apart(0) + take_apart(1)
        for copy in done:
            copy.wait()
        for s in (eg, eu):
            s.start(1)
        for s in expert:
            s.start(2)

        def block(r):
            held[r].wait()
            o = owner_dense(r)
            vectors = k.s_v[r]
            k.small[:, pl.ds(pl.multiple_of(o * 256, 256), 256)] = vectors
            normed = (cols(scaled, o, 256) * vectors[0:1, :].astype(f32)).astype(bf16)
            target = k.n_keep if r < 4 else k.n_send
            target[:, (r % 4) * 256 : (r % 4 + 1) * 256] = normed
            for m in range(3):
                acc[m] += dot_nn(normed, w[r, m * 256 : (m + 1) * 256, :])

        def arrived(r, onward=()):
            for s in first:
                s.wait(r)
                for t in onward:
                    s.start(t)
            bring(r)

        arrived(4)
        block(0)
        block(4)
        arrived(1, (3, 5))
        out.start(2)
        arrived(2, (6,))
        block(1)
        arrived(5)
        block(5)
        arrived(6)
        block(2)
        block(6)
        for copy in take_apart(2):
            copy.wait()
        for s in shared:
            s.start(1)
        for s in shared:
            s.start(4)
        ids_y.wait_recv()
        k.ids[0, 64:128, :] = k.ids_y[...]
        later.extend(to_z(lambda d: lambda: (k.ids.at[0], k.ids.at[d])))
        bring_out(0)
        out.wait(4)
        bring_out(4)
        out.wait(1)
        out.start(5)
        bring_out(1)
        arrived(3, (7,))
        block(3)
        arrived(7)
        block(7)
        for h in range(4):
            at = slice(h * 128, (h + 1) * 128)
            k.kv[0:256, at] = turn(acc[1, :, at], k.cs[...], k.sn[...]).astype(bf16)
        k.kv[256:512, :] = acc[2].astype(bf16)
        kv_y = wires.go(lambda: (k.kv, k.kv_oth), y_dev)
        out.start(3)
        sg.start(2)
        su.start(2)
        for h in range(4):
            at = slice(h * 128, (h + 1) * 128)
            k.q[:, at] = turn(acc[0, :, at], k.cs[...], k.sn[...]).astype(bf16)
        out.wait(5)
        bring_out(5)
        out.wait(2)
        out.start(6)
        bring_out(2)
        kv_y.wait_recv()
        mask_own = k.ids_near[0:1, :] <= k.ids_q[:, 0:1]
        mask_oth = k.ids_far[0:1, :] <= k.ids_q[:, 0:1]
        for h in range(4):
            at = slice(h * 128, (h + 1) * 128)
            w_own, w_oth = softmax_parts(
                k.q[:, at], k.kv[0:256, at], k.kv_oth[0:256, at], mask_own, mask_oth
            )
            value = dot_nn(w_own.astype(bf16), k.kv[256:512, at])
            value += dot_nn(w_oth.astype(bf16), k.kv_oth[256:512, at])
            k.low[:, at] = value.astype(bf16)
        out.wait(6)
        bring_out(6)
        out.wait(3)
        out.start(7)
        bring_out(3)
        out.wait(7)
        bring_out(7)
        for copy in held_out:
            copy.wait()
        for r in range(8):
            part = dot_nn(k.low[...], low_w[r]).astype(bf16)
            at = pl.ds(pl.multiple_of(owner_dense(r) * 256, 256), 256)
            for d in range(4):
                k.att_send[d, :, at] = part[d * 64 : (d + 1) * 64, :]

    pl.run_scoped(
        attention_part,
        pltpu.VMEM((256, 2048), f32),
        pltpu.VMEM((3, 256, 512), f32),
        pltpu.VMEM((8, 768, 512), bf16),
        pltpu.VMEM((8, 512, 256), bf16),
        pltpu.VMEM((3, 256, 2, 1408), bf16),
        pltpu.VMEM((3, 2, 256, 1408), bf16),
    )
    att_z = to_z(lambda d: lambda: (k.att_send.at[d], k.att.at[d - 1]))
    swap_n = wires.go(lambda: (k.n_send, k.n_x), core_dev)
    swap_low = wires.go(lambda: (k.low, k.low_x), core_dev)
    parts = SimpleNamespace(started=False)

    def expert_part(wg, wu, wd, slopes, acc, up, keep, send):
        group = []

        def gather(s, w):
            group.append(loads.go(s.block(0), w.at[0]))
            s.wait(2)
            group.append(loads.go(s.block(2), w.at[2]))
            s.wait(1)
            s.start(3)
            group.append(loads.go(s.block(1), w.at[1]))

        def gather_last(s, w):
            s.wait(3)
            group.append(loads.go(s.block(3), w.at[3]))

        gather(ed, wd)
        for copy in att_z:
            copy.wait_recv()
        value = piece(k.tok, 0, 64).astype(f32) + (
            k.att_send[0].astype(f32)
            + k.att[0].astype(f32)
            + k.att[1].astype(f32)
            + k.att[2].astype(f32)
        )
        inv = lax.rsqrt(jnp.mean(value * value, axis=-1, keepdims=True) + epsilon)
        k.hidden[...] = value
        k.rows[0:64, :] = (value * inv * k.small[1:2, :].astype(f32)).astype(bf16)
        own_y = wires.go(
            lambda: (k.rows.at[pl.ds(0, 64), :], k.rows.at[pl.ds(256, 64), :]), y_dev
        )
        g_y = wires.go(lambda: (k.g_own, k.g_oth), y_dev)
        sd.start(2)
        own_z = Collect(lambda d: k.rows.at[pl.ds(64 * d, 64), :])
        gather_last(ed, wd)
        gather(eg, wg)
        gather_last(eg, wg)
        for s in (sg, su):
            s.wait(2)
            s.start(6)
        own_z.hand_on()
        for copy in later:
            copy.wait_recv()
        own_y.wait_recv()
        own_z.wait()
        oth_z = to_z(
            lambda d: lambda: (
                k.rows.at[pl.ds(256, 64), :],
                k.rows.at[pl.ds(256 + 64 * d, 64), :],
            )
        )

        def g_piece(half, d, at):
            g = k.g_oth if half else k.g_own
            return g[pl.ds(pl.multiple_of(near(d) * 64, 64), 64), at].astype(f32)

        def route(half):
            chosen = []
            for d in range(4):
                named = (k.ids[d, half * 64 : (half + 1) * 64, :] == mine.astype(f32)).astype(f32)
                chosen.append(jnp.sum(named, axis=-1, keepdims=True))
            chosen = jnp.concatenate(chosen, axis=0)
            prob, lane = probabilities(k.rows[half * 256 : (half + 1) * 256, :], k.small)
            here = jnp.sum(jnp.where(lane == mine + 3, prob, 0.0), axis=-1, keepdims=True)
            gate = here * chosen
            for d in range(4):
                at = slice(half * 256 + d * 64, half * 256 + (d + 1) * 64)
                value = gate[d * 64 : (d + 1) * 64, :] * g_piece(half, d, slice(None))
                slopes[at, :] = value.astype(bf16)
            return gate, chosen

        def gate_part(half):
            rows_at = slice(half * 256, (half + 1) * 256)

            def one(r, _):
                at = pl.ds(pl.multiple_of(owner_expert(r) * 512, 512), 512)
                acc[0] += dot_nn(k.rows[rows_at, at], wg[r])
                acc[2] += dot_nt(slopes[rows_at, at], wd[r])
                return 0

            acc[...] = jnp.zeros_like(acc)
            lax.fori_loop(0, 4, one, 0)

        def phase_one(half):
            rows_at = slice(half * 256, (half + 1) * 256)

            def one(r, _):
                at = pl.ds(pl.multiple_of(owner_expert(r) * 512, 512), 512)
                acc[1] += dot_nn(k.rows[rows_at, at], wu[r])
                return 0

            lax.fori_loop(0, 4, one, 0)
            for d in range(4):
                at, to = slice(d * 64, (d + 1) * 64), slice(half * 256 + d * 64, half * 256 + (d + 1) * 64)
                act, gate_grad, up_grad = gated(acc[0, at, :], acc[1, at, :], acc[2, at, :])
                up[0, to, :] = act.astype(bf16)
                up[1, to, :] = gate_grad.astype(bf16)
                up[2, to, :] = up_grad.astype(bf16)

        lanes = lax.broadcasted_iota(jnp.int32, (64, 128), 1)

        def phase_two(half, gate, chosen, between):
            rows_at = slice(half * 256, (half + 1) * 256)

            def two(r, dgate):
                at = pl.ds(pl.multiple_of(owner_expert(r) * 512, 512), 512)
                result = dot_nn(up[0, rows_at, :], wd[r]).astype(bf16).astype(f32)
                grad = dot_nt(up[1, rows_at, :], wg[r]) + dot_nt(up[2, rows_at, :], wu[r])
                sums = []
                for d in range(4):
                    here = slice(d * 64, (d + 1) * 64)
                    g_rows = g_piece(half, d, at)
                    sums.append(jnp.sum(g_rows * result[here, :], axis=-1, keepdims=True))
                    part = gate[here, :] * result[here, :]
                    if half == 0:
                        k.out_sum[here, at] = part
                        k.grad_sum[here, at] = grad[here, :]
                    else:
                        k.e_out[d, :, at] = part.astype(bf16)
                        k.e_grad[d, :, at] = grad[here, :].astype(bf16)
                return dgate + jnp.concatenate(sums, axis=0)

            dgate = lax.fori_loop(0, 2, two, jnp.zeros((256, 1), f32))
            between()
            dgate = lax.fori_loop(2, 4, two, dgate) * chosen
            for d in range(4):
                extra = jnp.zeros((64, 128), f32)
                for m, part in enumerate(split3(dgate[d * 64 : (d + 1) * 64, :])):
                    extra = jnp.where(lanes == mine + 16 * m, part, extra)
                if half == 0:
                    k.extras[d * 64 : (d + 1) * 64, :] = extra
                else:
                    k.e_grad[d, :, 2048:2176] = extra.astype(bf16)

        gate, chosen = route(0)
        for copy in group:
            copy.wait()
        group.clear()
        gate_part(0)
        gather(eu, wu)
        gather_last(eu, wu)
        for copy in group:
            copy.wait()
        phase_one(0)
        phase_two(0, gate, chosen, lambda: None)
        sg.wait(1)
        sg.start(3)
        sg.start(5)
        for copy in oth_z + [g_y]:
            copy.wait_recv()
        gate, chosen = route(1)
        gate_part(1)
        phase_one(1)
        saved = [loads.go(up, k.ex_up)]
        for r in range(4):
            to = slice(r * 256, (r + 1) * 256)
            for target, m in ((keep, r), (send, r + 4)):
                at = pl.ds(pl.multiple_of(owner_dense(m) * 256, 256), 256)
                target[0:512, to] = slopes[:, at]
                target[512:1024, to] = k.rows[:, at]
        saved.append(loads.go(keep, k.ex_keep))
        swap_ex = wires.go(lambda: (send, k.ex_x), core_dev)
        sd.wait(2)
        sd.start(6)

        def pass_on():
            su.wait(1)
            su.start(3)
            su.start(5)

        phase_two(1, gate, chosen, pass_on)
        for copy in saved:
            copy.wait()
        swap_ex.wait_send()
        swap_ex.ends = lambda: (k.ex_keep, k.ex_x)
        parts.swap_ex = swap_ex

    pl.run_scoped(
        expert_part,
        pltpu.VMEM((4, 512, 1408), bf16),
        pltpu.VMEM((4, 512, 1408), bf16),
        pltpu.VMEM((4, 1408, 512), bf16),
        pltpu.VMEM((512, 2048), bf16),
        pltpu.VMEM((3, 256, 1408), f32),
        pltpu.VMEM((3, 512, 1408), bf16),
        pltpu.VMEM((1024, 1024), bf16),
        pltpu.VMEM((1024, 1024), bf16),
    )
    swap_up = {}
    for m in (1, 2, 0):
        swap_up[m] = wires.go(lambda m=m: (k.ex_up.at[m], k.ex_up_x.at[m]), core_dev)
    e_grad_z = to_z(lambda d: lambda: (k.e_grad.at[d], k.e_grad_z.at[d - 1]))
    e_out_z = to_z(lambda d: lambda: (k.e_out.at[d], k.e_out_z.at[d - 1]))
    over_y, over_x = {}, {}

    def expert_grad(m, kept, sent, landed):
        parts.swap_ex_wait()
        swap_up[m].wait_recv()

        def inner(left, right, keep, send):
            start = pl.ds(0 if m == 0 else 512, 512)
            got = [
                loads.go(k.ex_up.at[m], right.at[0]),
                loads.go(k.ex_up_x.at[m], right.at[1]),
                loads.go(k.ex_keep.at[start, :], left.at[0]),
                loads.go(k.ex_x.at[start, :], left.at[1]),
            ]
            for copy in got:
                copy.wait()
            saved = []
            for r in (3, 1, 2, 0):
                target = send if r % 2 else keep
                at = slice(r * 256, (r + 1) * 256)
                to = pl.ds(pl.multiple_of(((y + r // 2) % 2) * 256, 256), 256)
                if m == 0:
                    total = dot_tn(right[0], left[0, :, at]) + dot_tn(right[1], left[1, :, at])
                    target[:, to] = total.astype(bf16)
                else:
                    total = dot_tn(left[0, :, at], right[0]) + dot_tn(left[1, :, at], right[1])
                    target[to, :] = total.astype(bf16)
                if r == 1:
                    saved.append(loads.go(send, sent))
                if r == 2:
                    saved[0].wait()
                    over_x[6 + m] = wires.go(lambda: (sent, landed), x_dev)
            loads.go(keep, kept).wait()

        shape = (1408, 512) if m == 0 else (512, 1408)
        pl.run_scoped(
            inner,
            pltpu.VMEM((2, 512, 1024), bf16),
            pltpu.VMEM((2, 512, 1408), bf16),
            pltpu.VMEM(shape, bf16),
            pltpu.VMEM(shape, bf16),
        )

    def to_y(name, r, source, target):
        over_y[name, r] = wires.go(lambda: (source.at[r % 2], target.at[r % 2]), y_dev)

    def shared_grad(m, keep, send):
        def inner(left, right):
            if m == 0:
                got = [loads.go(k.sh_keep, left.at[0]), loads.go(k.sh_x, left.at[1])]
            else:
                start = pl.ds(512, 256)
                got = [
                    loads.go(k.ex_keep.at[start, :], left.at[0]),
                    loads.go(k.ex_x.at[start, :], left.at[1]),
                ]
            got.append(loads.go(k.sh_up.at[m], right.at[0]))
            got.append(loads.go(k.sh_up_x.at[m], right.at[1]))
            for copy in got:
                copy.wait()
            for r in (3, 1, 2, 0):
                target = send if r >= 2 else keep
                at = slice(r * 256, (r + 1) * 256)
                if m == 0:
                    total = dot_tn(right[0], left[0, :, at]) + dot_tn(right[1], left[1, :, at])
                else:
                    total = dot_tn(left[0, :, at], right[0]) + dot_tn(left[1, :, at], right[1])
                target[r % 2] = total.astype(bf16)

        pl.run_scoped(
            inner, pltpu.VMEM((2, 256, 1024), bf16), pltpu.VMEM((2, 256, 1408), bf16)
        )

    def swap_ex_wait():
        if not parts.started:
            parts.swap_ex.wait_recv()
            parts.started = True

    parts.swap_ex_wait = swap_ex_wait

    def shared_part(wg, wu, wd, slopes, acc, up, keep, send):
        routed = k.rows.at[pl.ds(0, 256), :]
        held = []

        def bring(r, group):
            for s in group:
                held.append(loads.go(s.block(r), {sg: wg, su: wu, sd: wd}[s].at[r]))

        def arrived(r, group, onward=()):
            for s in group:
                s.wait(r)
                for t in onward:
                    s.start(t)
            bring(r, group)

        def settle():
            for copy in held:
                copy.wait()
            held.clear()

        pair, last = (sg, su), (sd,)
        for r in (0, 1, 2):
            bring(r, pair)
        for r in (4, 6):
            arrived(r, pair)
        expert_grad(1, k.k_eg, k.t_eg, k.x_eg)
        arrived(5, pair)
        sd.wait(1)
        sd.start(3)
        sd.start(5)
        bring(0, last)
        bring(1, last)
        bring(2, last)
        arrived(4, last)
        arrived(6, last)
        arrived(5, last)
        wide = routed[...].astype(f32) * k.small[2:3, :].astype(f32)
        sw = jax.nn.sigmoid(jnp.sum(wide, axis=-1, keepdims=True))
        for d in range(4):
            at = slice(d * 64, (d + 1) * 64)
            slopes[at, :] = (sw[at, :] * piece(k.g_own, d, 64).astype(f32)).astype(bf16)
        for r in range(4):
            to = slice(r * 256, (r + 1) * 256)
            keep[:, to] = cols(slopes, owner_dense(r), 256)
            send[:, to] = cols(slopes, owner_dense(r + 4), 256)
        saved = [loads.go(keep, k.sh_keep), loads.go(send, k.sh_send)]
        acc[...] = jnp.zeros_like(acc)

        def one(j, _):
            r = j // 2 + (j % 2) * 4
            row = cols(routed, owner_dense(r), 256)
            acc[0] += dot_nn(row, wg[r])
            acc[1] += dot_nn(row, wu[r])
            return 0

        def back(j, _):
            r = j // 2 + (j % 2) * 4
            acc[2] += dot_nt(cols(slopes, owner_dense(r), 256), wd[r])
            return 0

        settle()
        lax.fori_loop(0, 6, one, 0)
        arrived(3, pair, (7,))
        arrived(7, pair)
        settle()
        lax.fori_loop(6, 8, one, 0)
        for d in range(4):
            at = slice(d * 64, (d + 1) * 64)
            up[0, at, :] = (jax.nn.silu(acc[0, at, :]) * acc[1, at, :]).astype(bf16)
        saved.append(loads.go(up.at[0], k.sh_up.at[0]))
        for copy in saved:
            copy.wait()
        swaps = [
            wires.go(lambda: (k.sh_up.at[0], k.sh_up_x.at[0]), core_dev),
            wires.go(lambda: (k.sh_send, k.sh_x), core_dev),
        ]
        lax.fori_loop(0, 6, back, 0)
        for copy in swaps:
            copy.wait_recv()
        shared_grad(0, k.k_sd, k.t_sd)
        to_y(2, 3, k.t_sd, k.y_sd)
        for copy in e_grad_z:
            copy.wait_recv()
        oth = k.e_grad[0].astype(f32)
        for d in range(3):
            oth += k.e_grad_z[d].astype(f32)
        k.g_send[...] = oth.astype(bf16)
        parts.grad_y = wires.go(lambda: (k.g_send, k.g_y), y_dev)
        expert_grad(2, k.k_eu, k.t_eu, k.x_eu)
        arrived(3, last, (7,))
        arrived(7, last)
        settle()
        lax.fori_loop(6, 8, back, 0)
        for d in range(4):
            at = slice(d * 64, (d + 1) * 64)
            _, gate_grad, up_grad = gated(acc[0, at, :], acc[1, at, :], acc[2, at, :])
            up[1, at, :] = gate_grad.astype(bf16)
            up[2, at, :] = up_grad.astype(bf16)
        saved = [loads.go(up.at[m], k.sh_up.at[m]) for m in (1, 2)]

        def two(r, slope):
            at = pl.ds(pl.multiple_of(owner_dense(r) * 256, 256), 256)
            part = dot_nn(up[0], wd[r])
            total = sw * part + k.out_sum[:, at]
            back = dot_nt(up[1], wg[r]) + dot_nt(up[2], wu[r]) + k.grad_sum[:, at]
            sums = []
            for d in range(4):
                rows_at = slice(d * 64, (d + 1) * 64)
                g_rows = k.g_own[pl.ds(pl.multiple_of(near(d) * 64, 64), 64), at].astype(f32)
                sums.append(jnp.sum(g_rows * part[rows_at, :], axis=-1, keepdims=True))
                k.s_out[d, :, at] = total[rows_at, :].astype(bf16)
                k.s_grad[d, :, at] = back[rows_at, :].astype(bf16)
            return slope + jnp.concatenate(sums, axis=0)

        slope = lax.fori_loop(0, 8, two, jnp.zeros((256, 1), f32))
        lanes = lax.broadcasted_iota(jnp.int32, (64, 128), 1)
        for d in range(4):
            rows_at = slice(d * 64, (d + 1) * 64)
            extra = k.extras[rows_at, :]
            for m, part in enumerate(split3(slope[rows_at, :])):
                extra = jnp.where(lanes == mine + 48 + 16 * m, part, extra)
            k.s_grad[d, :, 2048:2176] = extra.astype(bf16)
        for copy in saved:
            copy.wait()

    pl.run_scoped(
        shared_part,
        pltpu.VMEM((8, 256, 1408), bf16),
        pltpu.VMEM((8, 256, 1408), bf16),
        pltpu.VMEM((8, 1408, 256), bf16),
        pltpu.VMEM((256, 2048), bf16),
        pltpu.VMEM((3, 256, 1408), f32),
        pltpu.VMEM((3, 256, 1408), bf16),
        pltpu.VMEM((256, 1024), bf16),
        pltpu.VMEM((256, 1024), bf16),
    )
    swap_sh = [
        wires.go(lambda m=m: (k.sh_up.at[m], k.sh_up_x.at[m]), core_dev) for m in (1, 2)
    ]
    s_grad_z = to_z(lambda d: lambda: (k.s_grad.at[d], k.s_grad_z.at[d - 1]))

    def back_part(*refs):
        k_sg, k_su, k_q, k_o, k_v = refs[:5]
        t_sg, t_su, t_q, t_o, t_v = refs[5:10]
        f_sg, f_su, f_q, f_o, f_v, f_sd = refs[10:16]
        h_keep, h_send, h_x, lin, lin_x, vec, high, gkv, gkv_send, gn = refs[16:]
        k_sd, t_sd = k.k_sd, k.t_sd

        def fold(name, keep, landed, send, target, device=x_dev):
            over_y[name, 3].wait_recv()

            def inner(buffer):
                loads.go(landed.at[1], buffer).wait()
                send[...] = (keep[1].astype(f32) + buffer[...].astype(f32)).astype(bf16)

            pl.run_scoped(inner, pltpu.VMEM(tuple(keep.shape[1:]), bf16))
            over_x[name] = wires.go(lambda: (send, target), device)

        def finish_pair():
            for name in (0, 1):
                over_y[name, 2].wait_recv()
                over_x[name].wait_recv()

            def inner(left, right, total):
                got = [
                    loads.go(k.y_sg.at[0], left.at[0]),
                    loads.go(k.x_sg, right.at[0]),
                    loads.go(k.y_su.at[0], left.at[1]),
                    loads.go(k.x_su, right.at[1]),
                ]
                for copy in got:
                    copy.wait()
                for n, keep in enumerate((k_sg, k_su)):
                    value = keep[0].astype(f32) + left[n].astype(f32) + right[n].astype(f32)
                    total[:, n, :] = value.astype(bf16)
                loads.go(total, k.d_si).wait()

            pair = pltpu.VMEM((2, 256, 1408), bf16)
            pl.run_scoped(inner, pair, pair, pltpu.VMEM((256, 2, 1408), bf16))

        def finish(name, keep, landed, target, result):
            over_y[name, 2].wait_recv()

            def inner(left, right, total):
                got = loads.go(landed.at[0], left)
                over_x[name].wait_recv()
                more = loads.go(target, right)
                got.wait()
                more.wait()
                value = keep[0].astype(f32) + left[...].astype(f32) + right[...].astype(f32)
                total[...] = value.astype(total.dtype)
                loads.go(total, result).wait()

            shape = tuple(keep.shape[1:])
            pl.run_scoped(
                inner,
                pltpu.VMEM(shape, bf16),
                pltpu.VMEM(shape, bf16),
                pltpu.VMEM(shape, result.dtype),
            )

        swap_sh[0].wait_recv()
        shared_grad(1, k_sg, t_sg)
        to_y(0, 3, t_sg, k.y_sg)
        swap_sh[1].wait_recv()
        shared_grad(2, k_su, t_su)
        to_y(1, 3, t_su, k.y_su)
        expert_grad(0, k.k_ed, k.t_ed, k.x_ed)
        fold(2, k_sd, k.y_sd, f_sd, k.x_sd)

        def other_rows(buffer):
            for copy in e_out_z:
                copy.wait_recv()
            loads.go(k.e_out_z, buffer).wait()
            oth = k.e_out[0].astype(f32)
            for d in range(3):
                oth += buffer[d].astype(f32)
            k.o_send[...] = oth.astype(bf16)

        pl.run_scoped(other_rows, pltpu.VMEM((3, 64, 2048), bf16))
        for copy in s_grad_z:
            copy.wait_recv()
        parts.grad_y.wait_recv()
        total = k.s_grad[0].astype(f32) + k.g_y[...].astype(f32)
        for d in range(3):
            total += k.s_grad_z[d].astype(f32)
        own_rows(
            total,
            k.hidden[...],
            k.rows[0:64, :],
            piece(k.g_own, 0, 64),
            k.small,
            high,
            k.gh.at[0],
            vec,
        )
        gh_z = Collect(lambda d: k.gh.at[d])
        out_y = wires.go(lambda: (k.o_send, k.o_y), y_dev)
        to_y(2, 2, t_sd, k.y_sd)
        fold(0, k_sg, k.y_sg, f_sg, k.x_sg)
        gn_z, s_out_z = [], []

        def attention_back(w, o_w, acc, low_g):
            got, more = [loads.go(k.w_o, o_w.at[0])], [loads.go(k.w_q, w.at[0])]
            for r in range(1, 8):
                got.append(loads.go(k.s_o.at[r], o_w.at[r]))
                more.append(loads.go(k.s_q.at[r], w.at[r]))
            gh_z.hand_on()
            gh_z.wait()
            s_out_z.extend(to_z(lambda d: lambda: (k.s_out.at[d], k.s_out_z.at[d - 1])))
            for copy in got:
                copy.wait()
            acc[...] = jnp.zeros_like(acc)
            for r in range(8):
                at = pl.ds(pl.multiple_of(owner_dense(r) * 256, 256), 256)
                row = jnp.concatenate([k.gh[d, :, at] for d in range(4)], axis=0)
                target = h_keep if r < 4 else h_send
                target[:, (r % 4) * 256 : (r % 4 + 1) * 256] = row
                acc[...] += dot_nt(row, o_w[r])
            swap_h = wires.go(lambda: (h_send, k.h_x), core_dev)
            low_g[...] = acc[...].astype(bf16)
            mask_own = k.ids_near[0:1, :] <= k.ids_q[:, 0:1]
            mask_oth = k.ids_far[0:1, :] <= k.ids_q[:, 0:1]
            scale = 128 ** (-0.5)
            for h in range(4):
                at = slice(h * 128, (h + 1) * 128)
                w_own, w_oth = softmax_parts(
                    k.q[:, at], k.kv[0:256, at], k.kv_oth[0:256, at], mask_own, mask_oth
                )
                dw_own = dot_nt(low_g[:, at], k.kv[256:512, at])
                dw_oth = dot_nt(low_g[:, at], k.kv_oth[256:512, at])
                mean = jnp.sum(w_own * dw_own, axis=-1, keepdims=True)
                mean += jnp.sum(w_oth * dw_oth, axis=-1, keepdims=True)
                ds_own = (w_own * (dw_own - mean)).astype(bf16)
                ds_oth = (w_oth * (dw_oth - mean)).astype(bf16)
                gq = dot_nn(ds_own, k.kv[0:256, at]) + dot_nn(ds_oth, k.kv_oth[0:256, at])
                lin[0:256, at] = turn_back(gq * scale, k.cs[...], k.sn[...]).astype(bf16)
                gkv[0:256, at] = dot_tn(ds_own, k.q[:, at]) * scale
                gkv[256:512, at] = dot_tn(w_own.astype(bf16), low_g[:, at])
                gkv_send[0:256, at] = (dot_tn(ds_oth, k.q[:, at]) * scale).astype(bf16)
                gkv_send[256:512, at] = dot_tn(w_oth.astype(bf16), low_g[:, at]).astype(bf16)
            gkv_y = wires.go(lambda: (gkv_send, k.gkv_y), y_dev)
            to_y(0, 2, t_sg, k.y_sg)
            fold(1, k_su, k.y_su, f_su, k.x_su)
            for copy in more:
                copy.wait()
            gkv_y.wait_recv()
            for h in range(4):
                at = slice(h * 128, (h + 1) * 128)
                gk = gkv[0:256, at] + k.gkv_y[0:256, at].astype(f32)
                lin[256:512, at] = turn_back(gk, k.cs[...], k.sn[...]).astype(bf16)
            lin[512:768, :] = (gkv[256:512, :] + k.gkv_y[256:512, :].astype(f32)).astype(bf16)
            swap_lin = wires.go(lambda: (lin, k.lin_x), core_dev)
            for m in range(3):
                part = lin[m * 256 : (m + 1) * 256, :].astype(f32)
                vec[11 + m : 12 + m, 0:512] = jnp.sum(part, axis=0, keepdims=True)
            for r in range(8):
                at = pl.ds(pl.multiple_of(owner_dense(r) * 256, 256), 256)
                back = dot_nt(lin[0:256, :], w[r, 0:256, :])
                back += dot_nt(lin[256:512, :], w[r, 256:512, :])
                back += dot_nt(lin[512:768, :], w[r, 512:768, :])
                gain = jnp.zeros((1, 256), f32)
                for d in range(4):
                    rows_at = slice(d * 64, (d + 1) * 64)
                    t = k.tok[pl.ds(pl.multiple_of(near(d) * 64, 64), 64), at].astype(f32)
                    gain += jnp.sum(
                        back[rows_at, :] * t * k.inv1[rows_at, :], axis=0, keepdims=True
                    )
                    gn[d, :, at] = back[rows_at, :].astype(bf16)
                vec[0:1, at] = gain
            swap_vec = wires.go(lambda: (vec, k.vec_x), core_dev)
            gn_z.extend(to_z(lambda d: lambda: (gn.at[d], k.gn_z.at[d - 1])))
            for copy in (swap_h, swap_lin, swap_vec, swap_n, swap_low):
                copy.wait_recv()

        pl.run_scoped(
            attention_back,
            pltpu.VMEM((8, 768, 512), bf16),
            pltpu.VMEM((8, 512, 256), bf16),
            pltpu.VMEM((256, 512), f32),
            pltpu.VMEM((256, 512), bf16),
        )
        k.vec_x[...] += vec[...]
        line = lax.broadcasted_iota(jnp.int32, (16, 512), 0)

        def attention_grad(n_x, low_x):
            got = [
                loads.go(k.n_x, n_x),
                loads.go(k.low_x, low_x),
                loads.go(k.h_x, h_x),
                loads.go(k.lin_x, lin_x),
            ]
            for copy in got:
                copy.wait()

            def one(r):
                keep = r < 2
                b_q, b_v = (k_q, k_v) if keep else (t_q, t_v)
                at = slice(r * 256, (r + 1) * 256)
                left, left_x = k.n_keep[:, at], n_x[:, at]
                for m in range(3):
                    rows_at = slice(m * 256, (m + 1) * 256)
                    total = dot_tn(left, lin[rows_at, :]) + dot_tn(left_x, lin_x[rows_at, :])
                    b_q[r % 2, rows_at, :] = total.astype(bf16)
                total = dot_tn(k.low[...], h_keep[:, at]) + dot_tn(low_x[...], h_x[:, at])
                (t_o if r % 2 else k_o)[r // 2] = total.astype(bf16)
                here = cols(k.vec_x, owner_dense(r), 256)
                here = jnp.concatenate([here, jnp.zeros((16, 256), f32)], axis=1)
                b_v[r % 2] = jnp.where(line < 11, here, k.vec_x[:, 0:512]).astype(bf16)
                if not keep:
                    to_y(5, r, t_v, k.y_v)
                    to_y(3, r, t_q, k.y_q)
                if r % 2:
                    over_y[4, 2 + r // 2] = wires.go(
                        lambda: (t_o.at[r // 2], k.y_o.at[r // 2]), x_dev
                    )

            one(3)
            to_y(1, 2, t_su, k.y_su)
            one(1)
            one(2)
            one(0)

        pl.run_scoped(
            attention_grad, pltpu.VMEM((256, 1024), bf16), pltpu.VMEM((256, 512), bf16)
        )
        kept = [loads.go(k_q.at[0], k.keep_q), loads.go(k_o.at[0], k.keep_o)]

        def expert_finish(m, kept, landed, result):
            def inner(left, right):
                got = loads.go(kept, left)
                over_x[6 + m].wait_recv()
                more = loads.go(landed, right)
                got.wait()
                more.wait()
                left[...] = (left[...].astype(f32) + right[...].astype(f32)).astype(bf16)
                loads.go(left, result).wait()

            shape = pltpu.VMEM(tuple(result.shape), bf16)
            pl.run_scoped(inner, shape, shape)

        def expert_pair():
            for m in (1, 2):
                over_x[6 + m].wait_recv()

            def inner(left, right, total):
                for half in range(2):
                    at = pl.ds(256 * half, 256)
                    got = []
                    for n, (kept, landed) in enumerate(((k.k_eg, k.x_eg), (k.k_eu, k.x_eu))):
                        got.append(loads.go(kept.at[at, :], left.at[n]))
                        got.append(loads.go(landed.at[at, :], right.at[n]))
                    for copy in got:
                        copy.wait()
                    for n in range(2):
                        value = left[n].astype(f32) + right[n].astype(f32)
                        total[:, n, :] = value.astype(bf16)
                    loads.go(total, k.d_ei.at[at]).wait()

            pair = pltpu.VMEM((2, 256, 1408), bf16)
            pl.run_scoped(inner, pair, pair, pltpu.VMEM((256, 2, 1408), bf16))

        expert_pair()

        def outputs(s_z):
            for copy in s_out_z:
                copy.wait_recv()
            got = loads.go(k.s_out_z, s_z)
            for copy in gn_z:
                copy.wait_recv()
            grad = gn[0].astype(f32)
            for d in range(3):
                grad += k.gn_z[d].astype(f32)
            t = piece(k.tok, 0, 64).astype(f32)
            i = k.inv1[0:64, :]
            scaled = grad * k.small[0:1, :].astype(f32)
            mean = jnp.mean(scaled * t, axis=-1, keepdims=True)
            grad = high[...] + i * scaled - t * (i * i * i * mean)
            k.grad_tokens[...] = grad.astype(bf16)
            got.wait()
            total = k.hidden[...] + k.s_out[0].astype(f32)
            for d in range(3):
                total += s_z[d].astype(f32)
            out_y.wait_recv()
            k.output[...] = (total + k.o_y[...].astype(f32)).astype(bf16)

        expert_finish(0, k.k_ed, k.x_ed, k.d_ed)
        finish(2, k_sd, k.y_sd, k.x_sd, k.d_sd)
        fold(5, k_v, k.y_v, f_v, k.x_v)
        fold(3, k_q, k.y_q, f_q, k.x_q)
        fold(4, k_o, k.y_o, f_o, k.x_o, y_dev)
        pl.run_scoped(outputs, pltpu.VMEM((3, 64, 2048), bf16))
        finish_pair()
        finish(5, k_v, k.y_v, k.x_v, k.v_own)
        v_z = to_z(lambda d: lambda: (k.v_own, k.v_z.at[d - 1]))
        for name in (3, 4):
            over_y[name, 2].wait_recv()
            over_x[name].wait_recv()
        for copy in kept:
            copy.wait()
        for copy in v_z:
            copy.wait_recv()
        total = k.v_own[...] + k.v_z[0] + k.v_z[1] + k.v_z[2]
        k.d_v[...] = total[:, 0:256].astype(bf16)
        for h in range(4):
            lanes_at = slice(h * 128, (h + 1) * 128)
            turned = pltpu.roll(k.v_own[:, lanes_at], (128 - owner_dense(0) * 16) % 128, 1)
            for m in range(3):
                k.d_b[m, h : h + 1, :] = turned[11 + m : 12 + m, :].astype(bf16)
        wires.drain()

    def buffers(lead):
        return tuple(
            pltpu.VMEM(lead + shape, bf16)
            for shape in ((256, 1408), (256, 1408), (768, 512), (512, 256), (16, 512))
        )

    pl.run_scoped(
        back_part,
        *buffers((2,)),
        *buffers((2,)),
        *buffers(()),
        pltpu.VMEM((1408, 256), bf16),
        pltpu.VMEM((256, 1024), bf16),
        pltpu.VMEM((256, 1024), bf16),
        pltpu.VMEM((256, 1024), bf16),
        pltpu.VMEM((768, 512), bf16),
        pltpu.VMEM((768, 512), bf16),
        pltpu.VMEM((16, 2048), f32),
        pltpu.VMEM((64, 2048), f32),
        pltpu.VMEM((512, 512), f32),
        pltpu.VMEM((512, 512), bf16),
        pltpu.VMEM((4, 64, 2048), bf16),
    )


def close_kernel(k):
    loads = Loads(k.load_sems)
    sums = ((k.keep_q, k.y_q, k.x_q, k.b_q, k.c_q), (k.keep_o, k.y_o, k.x_o, k.b_o, k.c_o))
    parts = []
    for keep, y, x, buffer, _ in sums:
        parts.append([loads.go(a, buffer.at[n]) for n, a in enumerate((keep, y.at[0], x))])
    passed = (
        (k.d_ei, k.b_ei, k.c_ei),
        (k.d_ed, k.b_ed, k.c_ed),
        (k.d_si, k.b_si, k.c_si),
        (k.d_sd, k.b_sd, k.c_sd),
        (k.output, k.b_out, k.c_out),
        (k.grad_tokens, k.b_tok, k.c_tok),
    )
    got = [loads.go(source, buffer) for source, buffer, _ in passed]
    for m, target in enumerate((k.c_one, k.c_two, k.c_gate)):
        target[...] = k.d_v[m : m + 1, :].reshape(256)
    k.c_router[...] = k.d_v[3:11, :]
    k.c_bias[...] = k.d_b[:, :, 0:16]
    done = []
    for copies, (_, _, _, buffer, target) in zip(parts, sums):
        for copy in copies:
            copy.wait()
        total = buffer[0].astype(f32) + buffer[1].astype(f32) + buffer[2].astype(f32)
        buffer[0] = total.astype(bf16)
        done.append(loads.go(buffer.at[0], target))
    for copy, (_, buffer, target) in zip(got, passed):
        copy.wait()
        done.append(loads.go(buffer, target))
    for copy in done:
        copy.wait()


def dma(n):
    return pltpu.SemaphoreType.DMA((n,))


def fixed_body(
    tokens,
    norm1_gain,
    w_qkv,
    b_qkv,
    w_out,
    norm2_gain,
    w_router,
    shared_gate,
    w_shared_in,
    w_shared_out,
    w_expert_in,
    w_expert_out,
    block_ids,
    expert_ids,
    out_grad,
):
    tok, g_own = tokens[0], out_grad[0]
    rows = tok.shape[0]
    places = np.arange(2 * rows)[:, None]
    frequency = rope_base ** (-np.arange(64) / 64.0)
    cosine, sine = np.cos(places * frequency), np.sin(places * frequency)
    cs = np.concatenate([cosine, cosine], axis=1).astype(np.float32)
    sn = np.concatenate([-sine, sine], axis=1).astype(np.float32)

    def vm(*shape, kind=bf16):
        return pltpu.VMEM(shape, kind)

    def o(*shape, kind=bf16, at=A):
        return (shape, kind, at)

    w_q = w_qkv.transpose(1, 0, 2).reshape(768, 512)
    b = call(
        layer_kernel,
        0,
        dict(
            tok=(tok, V),
            g_own=(g_own, V),
            bias=(b_qkv, V),
            cs_all=(cs, V),
            sn_all=(sn, V),
            blocks=(block_ids, V),
            ids_own=(expert_ids[0].T, V),
            gain_one=(norm1_gain, V),
            gain_two=(norm2_gain, V),
            gate_vector=(shared_gate, V),
            router=(w_router.T, V),
            w_q=(w_q, A),
            w_o=(w_out, A),
            w_si=(w_shared_in, A),
            w_sd=(w_shared_out, A),
            w_ei=(w_expert_in[0], A),
            w_ed=(w_expert_out[0], A),
        ),
        dict(
            output=o(64, 2048, at=V),
            grad_tokens=o(64, 2048, at=V),
            d_v=o(16, 256, at=V),
            d_b=o(3, 4, 128, at=V),
            keep_q=o(768, 512),
            keep_o=o(512, 256),
            d_si=o(256, 2, 1408),
            d_sd=o(1408, 256),
            d_ei=o(512, 2, 1408),
            d_ed=o(1408, 512),
            split_si=o(2, 256, 1408),
            split_ei=o(2, 512, 1408),
            s_q=o(8, 768, 512),
            s_o=o(8, 512, 256),
            s_sg=o(8, 256, 1408),
            s_su=o(8, 256, 1408),
            s_sd=o(8, 1408, 256),
            s_eg=o(4, 512, 1408),
            s_eu=o(4, 512, 1408),
            s_ed=o(4, 1408, 512),
            ex_up=o(3, 512, 1408),
            ex_up_x=o(3, 512, 1408),
            ex_keep=o(1024, 1024),
            ex_x=o(1024, 1024),
            sh_up=o(3, 256, 1408),
            sh_up_x=o(3, 256, 1408),
            sh_keep=o(256, 1024),
            sh_send=o(256, 1024),
            sh_x=o(256, 1024),
            k_eg=o(512, 1408),
            k_eu=o(512, 1408),
            k_ed=o(1408, 512),
            t_eg=o(512, 1408),
            t_eu=o(512, 1408),
            t_ed=o(1408, 512),
            y_sg=o(2, 256, 1408),
            y_su=o(2, 256, 1408),
            y_sd=o(2, 1408, 256),
            y_q=o(2, 768, 512),
            y_o=o(2, 512, 256),
            y_v=o(2, 16, 512),
            x_sg=o(256, 1408),
            x_su=o(256, 1408),
            x_sd=o(1408, 256),
            x_q=o(768, 512),
            x_o=o(512, 256),
            x_v=o(16, 512),
            x_eg=o(512, 1408),
            x_eu=o(512, 1408),
            x_ed=o(1408, 512),
            n_x=o(256, 1024),
            low_x=o(256, 512),
            h_x=o(256, 1024),
            lin_x=o(768, 512),
            e_out_z=o(3, 64, 2048),
            s_out_z=o(3, 64, 2048),
        ),
        dict(
            s_v=vm(8, 16, 256),
            w_v=vm(16, 256),
            col=vm(512, 128, kind=f32),
            ids_q=vm(256, 128, kind=f32),
            ids_near=vm(8, 256, kind=f32),
            ids_far=vm(8, 256, kind=f32),
            cs=vm(256, 128, kind=f32),
            sn=vm(256, 128, kind=f32),
            ids=vm(4, 128, 128, kind=f32),
            ids_y=vm(64, 128, kind=f32),
            g_oth=vm(256, 2048),
            q=vm(256, 512),
            kv=vm(512, 512),
            kv_oth=vm(512, 512),
            low=vm(256, 512),
            n_keep=vm(256, 1024),
            n_send=vm(256, 1024),
            small=vm(16, 2048),
            inv1=vm(256, 1, kind=f32),
            k_sd=vm(2, 1408, 256),
            t_sd=vm(2, 1408, 256),
            att=vm(3, 64, 2048),
            att_send=vm(4, 64, 2048),
            hidden=vm(64, 2048, kind=f32),
            rows=vm(512, 2048),
            out_sum=vm(256, 2048, kind=f32),
            grad_sum=vm(256, 2048, kind=f32),
            extras=vm(256, 128, kind=f32),
            e_out=vm(4, 64, 2048),
            e_grad=vm(4, 64, 2176),
            e_grad_z=vm(3, 64, 2176),
            s_out=vm(4, 64, 2048),
            s_grad=vm(4, 64, 2176),
            s_grad_z=vm(3, 64, 2176),
            g_send=vm(64, 2176),
            g_y=vm(64, 2176),
            o_send=vm(64, 2048),
            o_y=vm(64, 2048),
            gh=vm(4, 64, 2048),
            gkv_y=vm(512, 512),
            gn_z=vm(3, 64, 2048),
            vec_x=vm(16, 2048, kind=f32),
            v_own=vm(16, 512, kind=f32),
            v_z=vm(3, 16, 512, kind=f32),
            send_sems=dma(128),
            recv_sems=dma(128),
            load_sems=dma(224),
        ),
        63,
        4 * 10**10,
        2 * 10**8,
    )
    c = call(
        close_kernel,
        None,
        dict(
            output=(b.output, A),
            grad_tokens=(b.grad_tokens, A),
            d_v=(b.d_v, V),
            d_b=(b.d_b, V),
            keep_q=(b.keep_q, A),
            y_q=(b.y_q, A),
            x_q=(b.x_q, A),
            keep_o=(b.keep_o, A),
            y_o=(b.y_o, A),
            x_o=(b.x_o, A),
            d_si=(b.d_si, A),
            d_sd=(b.d_sd, A),
            d_ei=(b.d_ei, A),
            d_ed=(b.d_ed, A),
        ),
        dict(
            c_out=o(64, 2048),
            c_tok=o(64, 2048),
            c_one=o(256, at=V),
            c_two=o(256, at=V),
            c_gate=o(256, at=V),
            c_router=o(8, 256, at=V),
            c_bias=o(3, 4, 16, at=V),
            c_q=o(768, 512),
            c_o=o(512, 256),
            c_si=o(256, 2, 1408),
            c_sd=o(1408, 256),
            c_ei=o(512, 2, 1408),
            c_ed=o(1408, 512),
        ),
        dict(
            b_out=vm(64, 2048),
            b_tok=vm(64, 2048),
            b_q=vm(3, 768, 512),
            b_o=vm(3, 512, 256),
            b_si=vm(256, 2, 1408),
            b_sd=vm(1408, 256),
            b_ei=vm(512, 2, 1408),
            b_ed=vm(1408, 512),
            load_sems=dma(32),
        ),
        63,
        10**6,
        2 * 10**7,
    )
    return (
        c.c_out[None],
        c.c_tok[None],
        c.c_one,
        c.c_q.reshape(3, 256, 512).transpose(1, 0, 2),
        c.c_bias,
        c.c_o,
        c.c_two,
        c.c_router.T,
        c.c_gate,
        c.c_si,
        c.c_sd,
        c.c_ei[None],
        c.c_ed[None],
    )


def solution(mesh):
    placed = (
        P(DP, CTX, None),
        P(PLANE),
        P(PLANE, None, EXP),
        P(None, EXP, None),
        P(EXP, PLANE),
        P(PLANE),
        P(PLANE, None),
        P(PLANE),
        P(PLANE, None, EXP),
        P(EXP, PLANE),
        P(GROUP, DP, None, None),
        P(GROUP, None, DP),
        P(DP, None),
        P(DP, GROUP, None),
        P(DP, CTX, None),
    )
    fixed = tuple(mesh.shape[a] for a in (DP, CTX, EXP)) == (4, 2, 4)
    return jax.shard_map(
        fixed_body if fixed else general_body,
        mesh=mesh,
        in_specs=placed,
        out_specs=(
            P(DP, GROUP, None),
            P(DP, GROUP, None),
            P(PLANE),
            P(PLANE, None, EXP),
            P(None, EXP, PLANE),
            P(EXP, PLANE),
            P(PLANE),
            P(PLANE, None),
            P(PLANE),
            P(PLANE, None, EXP),
            P(EXP, PLANE),
            P(GROUP, DP, None, None),
            P(GROUP, None, DP),
        ),
        check_vma=False,
    )
```

profile of v0, /device:TPU:0, one launch (start us, length us, event | category | flops | bytes accessed | tf_op | source)
XLA Modules:
  0.0 378.2 jit_solution(14137363748019654919)
XLA Ops:
  0.7 369.4 %shard_map.264 = (bf16[64,2048]{1,0:T(8,128)(2,1)}, bf16[64,2048]{1,0:T(8,128)(2,1)}, bf16[16,256]{1,0:T(8,128)(2,1)}, bf16[3,4,128]{2,1,0:T(4,128)(2,1)}, bf16[...) custom-call(bf16[256,2048]{1,0:T(8,128)(2,1)} %bitcast.23, ...), custom_call_target="tpu_custom_call" | custom-call | flops 40000000000 | bytes 200000000 | tf_op jit(solution)/shard_map/pallas_call | solution.py:645
  370.0 7.9 %shard_map.265 = (bf16[64,2048]{1,0:T(8,128)(2,1)}, bf16[64,2048]{1,0:T(8,128)(2,1)}, bf16[256]{0:T(256)(128)(2,1)}, bf16[256]{0:T(256)(128)(2,1)}, bf16[256]{0:...) custom-call(bf16[64,2048]{1,0:T(8,128)(2,1)} %get-tuple-element.40.r, ...), custom_call_target="tpu_custom_call" | custom-call | flops 1000000 | bytes 20000000 | tf_op jit(solution)/shard_map/pallas_call | solution.py:645
where the time goes:
time: 384 us; the launch traced here: 378 us
  Pallas kernels  377 us (98%)
    pallas_call x2, Pallas kernels, call(): pl.pallas_call(run, out_shape=tuple((jax.ShapeDtypeStruct(o[0], o[1]) for...  377 us

commit v1 on v0

--- a/solution.py
+++ b/solution.py
@@ -687,6 +687,15 @@
 def layer_kernel(k):
     x_dev, y_dev, core_dev, z_dev = peers()
     wires, loads = Wires(k.send_sems, k.recv_sems), Loads(k.load_sems)
+    inputs = [
+        loads.go(a, b)
+        for a, b in (
+            (k.tok_in, k.tok),
+            (k.cs_in, k.cs_all),
+            (k.sn_in, k.sn_all),
+            (k.g_in, k.g_own),
+        )
+    ]
     greet([x_dev, y_dev, core_dev] + z_dev)
     y = lax.axis_index(CTX)
     mine = y * 4 + lax.axis_index(EXP)
@@ -718,21 +727,24 @@
     su = Spread(wires, lambda: k.split_si.at[1], k.s_su, True)
     sd = Spread(wires, lambda: k.w_sd, k.s_sd, True)
     first, expert, shared = (vec, qkv), (eg, eu, ed), (sg, su, sd)
+    qkv.start(1)
+    qkv.start(2)
     k.w_v[...] = jnp.zeros_like(k.w_v)
     for m, vector in enumerate((k.gain_one, k.gain_two, k.gate_vector)):
         k.w_v[m : m + 1, :] = vector[...].reshape(1, 256)
     k.w_v[3:11, :] = k.router[...]
-    for s in first + (out, ed):
+    for s in (vec, out, ed):
         s.start(1)
-    for s in first:
-        s.start(2)
-    for s in first + (out,):
+    vec.start(2)
+    for s in (qkv, out, vec):
         s.start(4)
     k.col[0:128, :] = jnp.full((128, 128), -1.0, f32)
     k.col[0:4, 0:64] = k.ids_own[...].astype(f32)
     k.ids[0, 0:64, :] = k.col[0:128, :].T[0:64, :]
     ids_y = wires.go(lambda: (k.ids.at[0, pl.ds(0, 64), :], k.ids_y), y_dev)
     k.s_v[0] = k.w_v[...]
+    for copy in inputs:
+        copy.wait()
     k.col[...] = jnp.broadcast_to(k.blocks[...].astype(f32), (128, 512)).T
     for target, half in ((k.ids_near, y), (k.ids_far, 1 - y)):
         for d in range(4):
@@ -1128,10 +1140,18 @@
             pltpu.VMEM(shape, bf16),
         )
 
-    def to_y(name, r, source, target):
-        over_y[name, r] = wires.go(lambda: (source.at[r % 2], target.at[r % 2]), y_dev)
-
-    def shared_grad(m, keep, send):
+    def set_out(name, n, source, target, device):
+        over_y[name, n] = wires.go(lambda: (source.at[n], target.at[n]), device)
+
+    def y_first(name, keep, send, landed):
+        def store(r, total):
+            (send if r >= 2 else keep)[r % 2] = total
+            if r == 3:
+                set_out(name, 1, send, landed, y_dev)
+
+        return store
+
+    def shared_grad(m, store):
         def inner(left, right):
             if m == 0:
                 got = [loads.go(k.sh_keep, left.at[0]), loads.go(k.sh_x, left.at[1])]
@@ -1146,13 +1166,12 @@
             for copy in got:
                 copy.wait()
             for r in (3, 1, 2, 0):
-                target = send if r >= 2 else keep
                 at = slice(r * 256, (r + 1) * 256)
                 if m == 0:
                     total = dot_tn(right[0], left[0, :, at]) + dot_tn(right[1], left[1, :, at])
                 else:
                     total = dot_tn(left[0, :, at], right[0]) + dot_tn(left[1, :, at], right[1])
-                target[r % 2] = total.astype(bf16)
+                store(r, total.astype(bf16))
 
         pl.run_scoped(
             inner, pltpu.VMEM((2, 256, 1024), bf16), pltpu.VMEM((2, 256, 1408), bf16)
@@ -1210,7 +1229,7 @@
             to = slice(r * 256, (r + 1) * 256)
             keep[:, to] = cols(slopes, owner_dense(r), 256)
             send[:, to] = cols(slopes, owner_dense(r + 4), 256)
-        saved = [loads.go(keep, k.sh_keep), loads.go(send, k.sh_send)]
+        saved = [loads.go(keep, k.sh_keep)]
         acc[...] = jnp.zeros_like(acc)
 
         def one(j, _):
@@ -1234,18 +1253,18 @@
         for d in range(4):
             at = slice(d * 64, (d + 1) * 64)
             up[0, at, :] = (jax.nn.silu(acc[0, at, :]) * acc[1, at, :]).astype(bf16)
+        swaps = [
+            wires.go(lambda: (up.at[0], k.sh_up_x.at[0]), core_dev),
+            wires.go(lambda: (send, k.sh_x), core_dev),
+        ]
         saved.append(loads.go(up.at[0], k.sh_up.at[0]))
         for copy in saved:
             copy.wait()
-        swaps = [
-            wires.go(lambda: (k.sh_up.at[0], k.sh_up_x.at[0]), core_dev),
-            wires.go(lambda: (k.sh_send, k.sh_x), core_dev),
-        ]
         lax.fori_loop(0, 6, back, 0)
         for copy in swaps:
             copy.wait_recv()
-        shared_grad(0, k.k_sd, k.t_sd)
-        to_y(2, 3, k.t_sd, k.y_sd)
+            copy.wait_send()
+        shared_grad(0, y_first(2, k.k_sd, k.t_sd, k.y_sd))
         for copy in e_grad_z:
             copy.wait_recv()
         oth = k.e_grad[0].astype(f32)
@@ -1253,6 +1272,7 @@
             oth += k.e_grad_z[d].astype(f32)
         k.g_send[...] = oth.astype(bf16)
         parts.grad_y = wires.go(lambda: (k.g_send, k.g_y), y_dev)
+        set_out(2, 0, k.t_sd, k.y_sd, y_dev)
         expert_grad(2, k.k_eu, k.t_eu, k.x_eu)
         arrived(3, last, (7,))
         arrived(7, last)
@@ -1307,14 +1327,14 @@
     s_grad_z = to_z(lambda d: lambda: (k.s_grad.at[d], k.s_grad_z.at[d - 1]))
 
     def back_part(*refs):
-        k_sg, k_su, k_q, k_o, k_v = refs[:5]
-        t_sg, t_su, t_q, t_o, t_v = refs[5:10]
-        f_sg, f_su, f_q, f_o, f_v, f_sd = refs[10:16]
-        h_keep, h_send, h_x, lin, lin_x, vec, high, gkv, gkv_send, gn = refs[16:]
+        k_ga, k_gb, k_su, k_q, k_kv, k_o, k_v = refs[:7]
+        t_ga, t_gb, t_su, t_q, t_kv, t_o, t_v = refs[7:14]
+        f_ga, f_gb, f_su, f_q, f_kv, f_o, f_v, f_sd = refs[14:22]
+        h_keep, h_send, h_x, lin, lin_x, vec, high, gkv, gkv_send, gn = refs[22:]
         k_sd, t_sd = k.k_sd, k.t_sd
 
         def fold(name, keep, landed, send, target, device=x_dev):
-            over_y[name, 3].wait_recv()
+            over_y[name, 1].wait_recv()
 
             def inner(buffer):
                 loads.go(landed.at[1], buffer).wait()
@@ -1324,29 +1344,37 @@
             over_x[name] = wires.go(lambda: (send, target), device)
 
         def finish_pair():
-            for name in (0, 1):
-                over_y[name, 2].wait_recv()
+            for name in (0, 9, 1):
+                over_y[name, 0].wait_recv()
                 over_x[name].wait_recv()
 
             def inner(left, right, total):
+                first, last, whole = pl.ds(0, 128), pl.ds(128, 128), slice(0, 256)
                 got = [
-                    loads.go(k.y_sg.at[0], left.at[0]),
-                    loads.go(k.x_sg, right.at[0]),
+                    loads.go(k.y_ga.at[0], left.at[0, first, :]),
+                    loads.go(k.x_ga, right.at[0, first, :]),
+                    loads.go(k.y_gb.at[0], left.at[0, last, :]),
+                    loads.go(k.x_gb, right.at[0, last, :]),
                     loads.go(k.y_su.at[0], left.at[1]),
                     loads.go(k.x_su, right.at[1]),
                 ]
                 for copy in got:
                     copy.wait()
-                for n, keep in enumerate((k_sg, k_su)):
-                    value = keep[0].astype(f32) + left[n].astype(f32) + right[n].astype(f32)
-                    total[:, n, :] = value.astype(bf16)
+                for n, keep, at in (
+                    (0, k_ga, slice(0, 128)),
+                    (0, k_gb, slice(128, 256)),
+                    (1, k_su, whole),
+                ):
+                    value = keep[0].astype(f32) + left[n, at, :].astype(f32)
+                    value += right[n, at, :].astype(f32)
+                    total[at, n, :] = value.astype(bf16)
                 loads.go(total, k.d_si).wait()
 
             pair = pltpu.VMEM((2, 256, 1408), bf16)
             pl.run_scoped(inner, pair, pair, pltpu.VMEM((256, 2, 1408), bf16))
 
         def finish(name, keep, landed, target, result):
-            over_y[name, 2].wait_recv()
+            over_y[name, 0].wait_recv()
 
             def inner(left, right, total):
                 got = loads.go(landed.at[0], left)
@@ -1367,11 +1395,18 @@
             )
 
         swap_sh[0].wait_recv()
-        shared_grad(1, k_sg, t_sg)
-        to_y(0, 3, t_sg, k.y_sg)
+
+        def gate_store(r, total):
+            (t_ga if r >= 2 else k_ga)[r % 2] = total[0:128, :]
+            (t_gb if r % 2 else k_gb)[r // 2] = total[128:256, :]
+            if r == 3:
+                set_out(0, 1, t_ga, k.y_ga, y_dev)
+                set_out(9, 1, t_gb, k.y_gb, x_dev)
+
+        shared_grad(1, gate_store)
+        set_out(9, 0, t_gb, k.y_gb, x_dev)
         swap_sh[1].wait_recv()
-        shared_grad(2, k_su, t_su)
-        to_y(1, 3, t_su, k.y_su)
+        shared_grad(2, y_first(1, k_su, t_su, k.y_su))
         expert_grad(0, k.k_ed, k.t_ed, k.x_ed)
         fold(2, k_sd, k.y_sd, f_sd, k.x_sd)
 
@@ -1403,11 +1438,11 @@
         )
         gh_z = Collect(lambda d: k.gh.at[d])
         out_y = wires.go(lambda: (k.o_send, k.o_y), y_dev)
-        to_y(2, 2, t_sd, k.y_sd)
-        fold(0, k_sg, k.y_sg, f_sg, k.x_sg)
-        gn_z, s_out_z = [], []
-
-        def attention_back(w, o_w, acc, low_g):
+        fold(0, k_ga, k.y_ga, f_ga, k.x_ga)
+        fold(9, k_gb, k.y_gb, f_gb, k.x_gb, y_dev)
+        gn_z, s_out_z, vec_z = [], [], []
+
+        def attention_back(w, o_w, acc, low_g, n_x, low_x):
             got, more = [loads.go(k.w_o, o_w.at[0])], [loads.go(k.w_q, w.at[0])]
             for r in range(1, 8):
                 got.append(loads.go(k.s_o.at[r], o_w.at[r]))
@@ -1447,8 +1482,36 @@
                 gkv_send[0:256, at] = (dot_tn(ds_oth, k.q[:, at]) * scale).astype(bf16)
                 gkv_send[256:512, at] = dot_tn(w_oth.astype(bf16), low_g[:, at]).astype(bf16)
             gkv_y = wires.go(lambda: (gkv_send, k.gkv_y), y_dev)
-            to_y(0, 2, t_sg, k.y_sg)
+            swap_q = wires.go(
+                lambda: (lin.at[pl.ds(0, 256), :], k.lin_x.at[pl.ds(0, 256), :]), core_dev
+            )
+            set_out(0, 0, t_ga, k.y_ga, y_dev)
             fold(1, k_su, k.y_su, f_su, k.x_su)
+            for copy in (swap_h, swap_n, swap_low, swap_q):
+                copy.wait_recv()
+            got = [
+                loads.go(k.n_x, n_x),
+                loads.go(k.low_x, low_x),
+                loads.go(k.h_x, h_x),
+                loads.go(k.lin_x.at[pl.ds(0, 256), :], lin_x.at[pl.ds(0, 256), :]),
+            ]
+            for copy in got:
+                copy.wait()
+
+            def projection(r, m):
+                at, rows_at = slice(r * 256, (r + 1) * 256), slice(m * 256, (m + 1) * 256)
+                total = dot_tn(k.n_keep[:, at], lin[rows_at, :])
+                return (total + dot_tn(n_x[:, at], lin_x[rows_at, :])).astype(bf16)
+
+            for r in (3, 1, 2, 0):
+                at = slice(r * 256, (r + 1) * 256)
+                total = dot_tn(k.low[...], h_keep[:, at]) + dot_tn(low_x[...], h_x[:, at])
+                (t_o if r % 2 else k_o)[r // 2] = total.astype(bf16)
+                if r % 2:
+                    set_out(4, r // 2, t_o, k.y_o, x_dev)
+                (t_q if r >= 2 else k_q)[r % 2] = projection(r, 0)
+                if r == 3:
+                    set_out(3, 1, t_q, k.y_q, y_dev)
             for copy in more:
                 copy.wait()
             gkv_y.wait_recv()
@@ -1457,10 +1520,21 @@
                 gk = gkv[0:256, at] + k.gkv_y[0:256, at].astype(f32)
                 lin[256:512, at] = turn_back(gk, k.cs[...], k.sn[...]).astype(bf16)
             lin[512:768, :] = (gkv[256:512, :] + k.gkv_y[256:512, :].astype(f32)).astype(bf16)
-            swap_lin = wires.go(lambda: (lin, k.lin_x), core_dev)
+            swap_kv = wires.go(
+                lambda: (lin.at[pl.ds(256, 512), :], k.lin_x.at[pl.ds(256, 512), :]), core_dev
+            )
             for m in range(3):
                 part = lin[m * 256 : (m + 1) * 256, :].astype(f32)
                 vec[11 + m : 12 + m, 0:512] = jnp.sum(part, axis=0, keepdims=True)
+            swap_kv.wait_recv()
+            loads.go(k.lin_x.at[pl.ds(256, 512), :], lin_x.at[pl.ds(256, 512), :]).wait()
+            for r in (3, 2, 1, 0):
+                target = t_kv if r >= 2 else k_kv
+                for m in (1, 2):
+                    target[r % 2, (m - 1) * 256 : m * 256, :] = projection(r, m)
+                if r == 3:
+                    set_out(10, 1, t_kv, k.y_kv, y_dev)
+                    set_out(1, 0, t_su, k.y_su, y_dev)
             for r in range(8):
                 at = pl.ds(pl.multiple_of(owner_dense(r) * 256, 256), 256)
                 back = dot_nt(lin[0:256, :], w[r, 0:256, :])
@@ -1475,10 +1549,8 @@
                     )
                     gn[d, :, at] = back[rows_at, :].astype(bf16)
                 vec[0:1, at] = gain
-            swap_vec = wires.go(lambda: (vec, k.vec_x), core_dev)
+            vec_z.extend(to_z(lambda d: lambda: (vec, k.vec_z.at[d - 1])))
             gn_z.extend(to_z(lambda d: lambda: (gn.at[d], k.gn_z.at[d - 1])))
-            for copy in (swap_h, swap_lin, swap_vec, swap_n, swap_low):
-                copy.wait_recv()
 
         pl.run_scoped(
             attention_back,
@@ -1486,53 +1558,11 @@
             pltpu.VMEM((8, 512, 256), bf16),
             pltpu.VMEM((256, 512), f32),
             pltpu.VMEM((256, 512), bf16),
+            pltpu.VMEM((256, 1024), bf16),
+            pltpu.VMEM((256, 512), bf16),
         )
-        k.vec_x[...] += vec[...]
-        line = lax.broadcasted_iota(jnp.int32, (16, 512), 0)
-
-        def attention_grad(n_x, low_x):
-            got = [
-                loads.go(k.n_x, n_x),
-                loads.go(k.low_x, low_x),
-                loads.go(k.h_x, h_x),
-                loads.go(k.lin_x, lin_x),
-            ]
-            for copy in got:
-                copy.wait()
-
-            def one(r):
-                keep = r < 2
-                b_q, b_v = (k_q, k_v) if keep else (t_q, t_v)
-                at = slice(r * 256, (r + 1) * 256)
-                left, left_x = k.n_keep[:, at], n_x[:, at]
-                for m in range(3):
-                    rows_at = slice(m * 256, (m + 1) * 256)
-                    total = dot_tn(left, lin[rows_at, :]) + dot_tn(left_x, lin_x[rows_at, :])
-                    b_q[r % 2, rows_at, :] = total.astype(bf16)
-                total = dot_tn(k.low[...], h_keep[:, at]) + dot_tn(low_x[...], h_x[:, at])
-                (t_o if r % 2 else k_o)[r // 2] = total.astype(bf16)
-                here = cols(k.vec_x, owner_dense(r), 256)
-                here = jnp.concatenate([here, jnp.zeros((16, 256), f32)], axis=1)
-                b_v[r % 2] = jnp.where(line < 11, here, k.vec_x[:, 0:512]).astype(bf16)
-                if not keep:
-                    to_y(5, r, t_v, k.y_v)
-                    to_y(3, r, t_q, k.y_q)
-                if r % 2:
-                    over_y[4, 2 + r // 2] = wires.go(
-                        lambda: (t_o.at[r // 2], k.y_o.at[r // 2]), x_dev
-                    )
-
-            one(3)
-            to_y(1, 2, t_su, k.y_su)
-            one(1)
-            one(2)
-            one(0)
-
-        pl.run_scoped(
-            attention_grad, pltpu.VMEM((256, 1024), bf16), pltpu.VMEM((256, 512), bf16)
-        )
-        kept = [loads.go(k_q.at[0], k.keep_q), loads.go(k_o.at[0], k.keep_o)]
-
+        kept = [loads.go(k_q.at[0], k.keep_q), loads.go(k_kv.at[0], k.keep_kv)]
+        kept.append(loads.go(k_o.at[0], k.keep_o))
         def expert_finish(m, kept, landed, result):
             def inner(left, right):
                 got = loads.go(kept, left)
@@ -1568,6 +1598,25 @@
             pl.run_scoped(inner, pair, pair, pltpu.VMEM((256, 2, 1408), bf16))
 
         expert_pair()
+        for copy in vec_z:
+            copy.wait_recv()
+        line = lax.broadcasted_iota(jnp.int32, (16, 2048), 0)
+        over_z = k.vec_z[0] + k.vec_z[1] + k.vec_z[2]
+        k.vec_sum[...] = vec[...] + jnp.where(line < 11, over_z, 0.0)
+        swap_vec = wires.go(lambda: (k.vec_sum, k.vec_x), core_dev)
+        swap_vec.wait_recv()
+        k.vec_x[...] += k.vec_sum[...]
+        line = lax.broadcasted_iota(jnp.int32, (16, 512), 0)
+        for r in (3, 2, 1, 0):
+            here = cols(k.vec_x, owner_dense(r), 256)
+            here = jnp.concatenate([here, jnp.zeros((16, 256), f32)], axis=1)
+            here = jnp.where(line < 11, here, k.vec_x[:, 0:512]).astype(bf16)
+            (t_v if r >= 2 else k_v)[r % 2] = here
+            if r >= 2:
+                set_out(5, r % 2, t_v, k.y_v, y_dev)
+        kept.append(loads.go(k_v.at[0], k.keep_v))
+        set_out(3, 0, t_q, k.y_q, y_dev)
+        set_out(10, 0, t_kv, k.y_kv, y_dev)
 
         def outputs(s_z):
             for copy in s_out_z:
@@ -1593,33 +1642,25 @@
 
         expert_finish(0, k.k_ed, k.x_ed, k.d_ed)
         finish(2, k_sd, k.y_sd, k.x_sd, k.d_sd)
+        fold(3, k_q, k.y_q, f_q, k.x_q)
+        fold(10, k_kv, k.y_kv, f_kv, k.x_kv)
         fold(5, k_v, k.y_v, f_v, k.x_v)
-        fold(3, k_q, k.y_q, f_q, k.x_q)
         fold(4, k_o, k.y_o, f_o, k.x_o, y_dev)
         pl.run_scoped(outputs, pltpu.VMEM((3, 64, 2048), bf16))
         finish_pair()
-        finish(5, k_v, k.y_v, k.x_v, k.v_own)
-        v_z = to_z(lambda d: lambda: (k.v_own, k.v_z.at[d - 1]))
-        for name in (3, 4):
-            over_y[name, 2].wait_recv()
+        for name in (3, 10, 4, 5):
+            over_y[name, 0].wait_recv()
             over_x[name].wait_recv()
         for copy in kept:
             copy.wait()
-        for copy in v_z:
-            copy.wait_recv()
-        total = k.v_own[...] + k.v_z[0] + k.v_z[1] + k.v_z[2]
-        k.d_v[...] = total[:, 0:256].astype(bf16)
-        for h in range(4):
-            lanes_at = slice(h * 128, (h + 1) * 128)
-            turned = pltpu.roll(k.v_own[:, lanes_at], (128 - owner_dense(0) * 16) % 128, 1)
-            for m in range(3):
-                k.d_b[m, h : h + 1, :] = turned[11 + m : 12 + m, :].astype(bf16)
         wires.drain()
+
+    shapes = [(128, 1408), (128, 1408), (256, 1408), (256, 512), (512, 512), (512, 256), (16, 512)]
 
     def buffers(lead):
         return tuple(
             pltpu.VMEM(lead + shape, bf16)
-            for shape in ((256, 1408), (256, 1408), (768, 512), (512, 256), (16, 512))
+            for shape in shapes
         )
 
     pl.run_scoped(
@@ -1643,7 +1684,11 @@
 
 def close_kernel(k):
     loads = Loads(k.load_sems)
-    sums = ((k.keep_q, k.y_q, k.x_q, k.b_q, k.c_q), (k.keep_o, k.y_o, k.x_o, k.b_o, k.c_o))
+    sums = (
+        (k.keep_q, k.y_q, k.x_q, k.b_q, k.c_q.at[pl.ds(0, 256), :]),
+        (k.keep_kv, k.y_kv, k.x_kv, k.b_kv, k.c_q.at[pl.ds(256, 512), :]),
+        (k.keep_o, k.y_o, k.x_o, k.b_o, k.c_o),
+    )
     parts = []
     for keep, y, x, buffer, _ in sums:
         parts.append([loads.go(a, buffer.at[n]) for n, a in enumerate((keep, y.at[0], x))])
@@ -1656,10 +1701,17 @@
         (k.grad_tokens, k.b_tok, k.c_tok),
     )
     got = [loads.go(source, buffer) for source, buffer, _ in passed]
+    total = k.keep_v[...].astype(f32) + k.y_v[0].astype(f32) + k.x_v[...].astype(f32)
+    low = total.astype(bf16)
     for m, target in enumerate((k.c_one, k.c_two, k.c_gate)):
-        target[...] = k.d_v[m : m + 1, :].reshape(256)
-    k.c_router[...] = k.d_v[3:11, :]
-    k.c_bias[...] = k.d_b[:, :, 0:16]
+        target[...] = low[m : m + 1, 0:256].reshape(256)
+    k.c_router[...] = low[3:11, 0:256]
+    for h in range(4):
+        here = pltpu.roll(
+            total[:, h * 128 : (h + 1) * 128], (128 - owner_dense(0) * 16) % 128, 1
+        )
+        for m in range(3):
+            k.c_bias[m, h : h + 1, :] = here[11 + m : 12 + m, 0:16].astype(bf16)
     done = []
     for copies, (_, _, _, buffer, target) in zip(parts, sums):
         for copy in copies:
@@ -1714,11 +1766,11 @@
         layer_kernel,
         0,
         dict(
-            tok=(tok, V),
-            g_own=(g_own, V),
+            tok_in=(tok, A),
+            g_in=(g_own, A),
             bias=(b_qkv, V),
-            cs_all=(cs, V),
-            sn_all=(sn, V),
+            cs_in=(cs, A),
+            sn_in=(sn, A),
             blocks=(block_ids, V),
             ids_own=(expert_ids[0].T, V),
             gain_one=(norm1_gain, V),
@@ -1735,9 +1787,9 @@
         dict(
             output=o(64, 2048, at=V),
             grad_tokens=o(64, 2048, at=V),
-            d_v=o(16, 256, at=V),
-            d_b=o(3, 4, 128, at=V),
-            keep_q=o(768, 512),
+            keep_v=o(16, 512),
+            keep_q=o(256, 512),
+            keep_kv=o(512, 512),
             keep_o=o(512, 256),
             d_si=o(256, 2, 1408),
             d_sd=o(1408, 256),
@@ -1760,7 +1812,6 @@
             sh_up=o(3, 256, 1408),
             sh_up_x=o(3, 256, 1408),
             sh_keep=o(256, 1024),
-            sh_send=o(256, 1024),
             sh_x=o(256, 1024),
             k_eg=o(512, 1408),
             k_eu=o(512, 1408),
@@ -1768,16 +1819,20 @@
             t_eg=o(512, 1408),
             t_eu=o(512, 1408),
             t_ed=o(1408, 512),
-            y_sg=o(2, 256, 1408),
+            y_ga=o(2, 128, 1408),
+            y_gb=o(2, 128, 1408),
             y_su=o(2, 256, 1408),
             y_sd=o(2, 1408, 256),
-            y_q=o(2, 768, 512),
+            y_q=o(2, 256, 512),
+            y_kv=o(2, 512, 512),
             y_o=o(2, 512, 256),
             y_v=o(2, 16, 512),
-            x_sg=o(256, 1408),
+            x_ga=o(128, 1408),
+            x_gb=o(128, 1408),
             x_su=o(256, 1408),
             x_sd=o(1408, 256),
-            x_q=o(768, 512),
+            x_q=o(256, 512),
+            x_kv=o(512, 512),
             x_o=o(512, 256),
             x_v=o(16, 512),
             x_eg=o(512, 1408),
@@ -1792,6 +1847,10 @@
         ),
         dict(
             s_v=vm(8, 16, 256),
+            tok=vm(256, 2048),
+            g_own=vm(256, 2048),
+            cs_all=vm(512, 128, kind=f32),
+            sn_all=vm(512, 128, kind=f32),
             w_v=vm(16, 256),
             col=vm(512, 128, kind=f32),
             ids_q=vm(256, 128, kind=f32),
@@ -1833,10 +1892,10 @@
             gkv_y=vm(512, 512),
             gn_z=vm(3, 64, 2048),
             vec_x=vm(16, 2048, kind=f32),
-            v_own=vm(16, 512, kind=f32),
-            v_z=vm(3, 16, 512, kind=f32),
-            send_sems=dma(128),
-            recv_sems=dma(128),
+            vec_z=vm(3, 16, 2048, kind=f32),
+            vec_sum=vm(16, 2048, kind=f32),
+            send_sems=dma(144),
+            recv_sems=dma(144),
             load_sems=dma(224),
         ),
         63,
@@ -1849,11 +1908,15 @@
         dict(
             output=(b.output, A),
             grad_tokens=(b.grad_tokens, A),
-            d_v=(b.d_v, V),
-            d_b=(b.d_b, V),
+            keep_v=(b.keep_v, V),
+            y_v=(b.y_v, V),
+            x_v=(b.x_v, V),
             keep_q=(b.keep_q, A),
             y_q=(b.y_q, A),
             x_q=(b.x_q, A),
+            keep_kv=(b.keep_kv, A),
+            y_kv=(b.y_kv, A),
+            x_kv=(b.x_kv, A),
             keep_o=(b.keep_o, A),
             y_o=(b.y_o, A),
             x_o=(b.x_o, A),
@@ -1880,7 +1943,8 @@
         dict(
             b_out=vm(64, 2048),
             b_tok=vm(64, 2048),
-            b_q=vm(3, 768, 512),
+            b_q=vm(3, 256, 512),
+            b_kv=vm(3, 512, 512),
             b_o=vm(3, 512, 256),
             b_si=vm(256, 2, 1408),
             b_sd=vm(1408, 256),

time: 384 us -> 376 us (0.979)
  Pallas kernels: 377 us -> 370 us
    pallas_call x2, Pallas kernels: 377 us -> 370 us  [call(): pl.pallas_call(run, out_shape=tuple((jax.ShapeDtypeStruct(o[0], o[1]) for...]
where the time goes in v1:
time: 376 us; the launch traced here: 371 us
  Pallas kernels  370 us (98%)
    pallas_call x2, Pallas kernels, call(): pl.pallas_call(run, out_shape=tuple((jax.ShapeDtypeStruct(o[0], o[1]) for...  370 us

profile of v1, /device:TPU:0, one launch (start us, length us, event | category | flops | bytes accessed | tf_op | source)
XLA Modules:
  0.0 371.1 jit_solution(417343105393636096)
XLA Ops:
  0.7 362.6 %shard_map.264 = (bf16[64,2048]{1,0:T(8,128)(2,1)}, bf16[64,2048]{1,0:T(8,128)(2,1)}, bf16[16,512]{1,0:T(8,128)(2,1)}, bf16[256,512]{1,0:T(8,128)(2,1)}, bf16[51...) custom-call(bf16[256,2048]{1,0:T(8,128)(2,1)} %bitcast.23, ...), custom_call_target="tpu_custom_call" | custom-call | flops 40000000000 | bytes 200000000 | tf_op jit(solution)/shard_map/pallas_call | solution.py:645
  363.2 7.6 %shard_map.265 = (bf16[64,2048]{1,0:T(8,128)(2,1)}, bf16[64,2048]{1,0:T(8,128)(2,1)}, bf16[256]{0:T(256)(128)(2,1)}, bf16[256]{0:T(256)(128)(2,1)}, bf16[256]{0:...) custom-call(bf16[64,2048]{1,0:T(8,128)(2,1)} %get-tuple-element.44.r, ...), custom_call_target="tpu_custom_call" | custom-call | flops 1000000 | bytes 20000000 | tf_op jit(solution)/shard_map/pallas_call | solution.py:645
